TPU v7x, 256 devices: a whole 4x4x8 slice. The times are simulated.
256 devices in a mesh: ctx: 64 (over z, x, core), head: 4 (over y).
Axes of the slice: x: 4, y: 4, z: 8, core: 2. Of those that a mesh axis runs over, the one named last changes fastest.
Arguments:
- query_rows: bfloat16 [32768, 4096], P('ctx', 'head'), may hold values from -1.75 to 1.75
- key_rows: bfloat16 [32768, 4096], P('ctx', 'head'), may hold values from -1.75 to 1.75
- value_rows: bfloat16 [32768, 4096], P('ctx', 'head'), may hold values from -6 to 6
- gate_rows: bfloat16 [32768, 4096], P('ctx', 'head'), may hold values from -8 to 8
- init_state: float32 [32, 128, 128], P('head'), may hold values from -192 to 192
- decay_rate: float32 [32], P('head'), as said below
- norm_gain: float32 [4096], P('head'), may hold values from 0.1 to 1.9
- out_weight: bfloat16 [4096, 6144], P('head', 'ctx'), may hold values from -0.25 to 0.25
Outputs:
- mixed: bfloat16 [32768, 6144], P('ctx', 'head')
Inputs may be any that keep to these rules, and one draw needn't show every extreme that they name: `decay_rate`: each rate is positive, between 0.05 / 32768 and 1/30.
All inputs are finite; a program needn't handle non-finite values.
Results may differ from a plain program's by a relative error of at most 0.015.
Values may be sent and summed in bfloat16 or wider, within the bound.
A program may use at most 128 MiB of HBM per device.

v0:
```python
import jax
import jax.numpy as jnp
from jax import lax
from jax.sharding import PartitionSpec as P

BLOCK = 256


def entering(part, axis, combine, identity):
    place = lax.axis_index(axis)
    gathered = jax.tree.map(lambda a: lax.all_gather(a, axis), part)
    state = jax.tree.map(lambda a, e: jnp.zeros_like(a) + jnp.asarray(e, a.dtype), part, identity)

    def one(lap, state):
        return combine(
            state, jax.tree.map(lambda a: lax.dynamic_index_in_dim(a, lap, 0, False), gathered)
        )

    return lax.fori_loop(0, place, one, state)


def combine(earlier, later):
    return (earlier[0] * later[0], later[0][:, None, None] * earlier[1] + later[1])


def body(
    query_rows, key_rows, value_rows, gate_rows, init_state, decay_rate, norm_gain, out_weight
):
    row_count, width = query_rows.shape
    head_dim = init_state.shape[1]
    head_count = width // head_dim
    block_len = BLOCK
    block_count = row_count // block_len
    highest = lax.Precision.HIGHEST
    shape_four = (block_count, block_len, head_count, head_dim)
    query_blocks = query_rows.reshape(shape_four)
    key_blocks = key_rows.reshape(shape_four)
    value_blocks = value_rows.reshape(shape_four)
    position = jnp.arange(block_len, dtype=jnp.float32)
    offset = position[:, None] - position[None, :]
    decay_mat = jnp.where(
        offset[None] >= 0.0,
        jnp.exp(-decay_rate[:, None, None] * jnp.maximum(offset, 0.0)[None]),
        0.0,
    )
    into_weight = jnp.exp(-decay_rate[None, :] * (position[:, None] + 1.0))
    key_weight = jnp.exp(-decay_rate[None, :] * (block_len - 1.0 - position)[:, None])
    block_decay = jnp.exp(-decay_rate * block_len)
    keyed = key_blocks.astype(jnp.float32) * key_weight[None, :, :, None]
    contribs = jnp.einsum(
        "njhd,njhe->nhde", keyed, value_blocks.astype(jnp.float32), precision=highest
    )
    local_sum = contribs[0]
    block_id = 1
    local_sum = block_decay[:, None, None] * local_sum + contribs[block_id]
    span_decay = jnp.exp(-decay_rate * row_count)
    identity = (
        jnp.ones((head_count,), jnp.float32),
        jnp.zeros((head_count, head_dim, head_dim), jnp.float32),
    )
    prior_decay, prior_sum = entering((span_decay, local_sum), "ctx", combine, identity)
    incoming = prior_decay[:, None, None] * init_state + prior_sum
    scores = jnp.einsum(
        "nihd,njhd->nhij", query_blocks, key_blocks, preferred_element_type=jnp.float32
    )
    weights_bf = (scores * decay_mat[None]).astype(jnp.bfloat16)
    intra = jnp.einsum(
        "nhij,njhd->nihd", weights_bf, value_blocks, preferred_element_type=jnp.float32
    )
    state = incoming
    inter_list = []
    for block_id in range(block_count):
        inter_blk = jnp.einsum(
            "ihd,hde->ihe", query_blocks[block_id].astype(jnp.float32), state, precision=highest
        )
        inter_list.append(inter_blk * into_weight[:, :, None])
        state = block_decay[:, None, None] * state + contribs[block_id]
    attn = intra + jnp.stack(inter_list, axis=0)
    scale = lax.rsqrt(jnp.mean(attn * attn, axis=-1, keepdims=True) + 1e-06)
    normed = (attn * scale).reshape(row_count, width)
    hidden = (normed * norm_gain[None, :] * jax.nn.sigmoid(gate_rows.astype(jnp.float32))).astype(
        jnp.bfloat16
    )
    terms = jnp.dot(
        hidden,
        lax.all_gather(out_weight, "ctx", axis=1, tiled=True),
        preferred_element_type=jnp.float32,
    )
    summed = lax.psum_scatter(terms.astype(jnp.bfloat16), "head", scatter_dimension=1, tiled=True)
    return summed


def solution(mesh):
    return jax.shard_map(
        body,
        mesh=mesh,
        in_specs=(
            P("ctx", "head"),
            P("ctx", "head"),
            P("ctx", "head"),
            P("ctx", "head"),
            P("head", None, None),
            P("head"),
            P("head"),
            P("head", "ctx"),
        ),
        out_specs=P("ctx", "head"),
        check_vma=False,
    )
```

profile of v0, /device:TPU:129, one launch (start us, length us, event | category | flops | bytes accessed | tf_op | source)
XLA Modules:
  0.0 331.4 jit_solution(17506133854481306700)
XLA Ops:
  6.5 1.6 copy.43
  10.6 1.4 fusion.2
  14.7 126.1 %all-reduce = f32[512]{0:T(512)S(1)} all-reduce(f32[512]{0:T(512)S(1)} %get-tuple-element.57), channel_id=2, replica_groups=mesh['ctx'=64,'head'=4] {'ctx'}, use_global_device_ids=true, to_apply=%add | all-reduce | flops 512 | bytes 4096
  142.0 2.2 copy.41
  144.2 2.0 copy.40
  146.2 1.3 copy.42
  147.6 1.7 exponential_select_fusion
  149.3 7.0 %all-gather.4.cloned.1.call-done = f32[64,8,128,128]{3,2,1,0:T(8,128)} async-done(((f32[1,8,128,128]{3,2,1,0:T(8,128)}), f32[64,8,128,128]{3,2,1,0:T(8,128)}) %all-gather.4.cloned.1.call-update) | async-done | bytes 33554448 | tf_op jit(solution)/shard_map/all_gather | solution.py:11
  156.4 41.0 %while.12 = (s32[]{:T(128)}, f32[8]{0:T(128)S(1)}, f32[8,128,128]{2,1,0:T(8,128)S(1)}, s32[]{:T(128)}, f32[64,8]{1,0:T(8,128)S(1)}, /*index=5*/f32[64,8,128,128]{3,2,1,0:T(8,128)}, s32[]{:T(128)}, s32[]{:T(128)}, s32[]{:T(128)}) while((s32[]{:T(128)}, f32[8]{0:T(128)S(1)}, f32[8,128,128]{2,1,0:T(8,128)S(1)}, s32[]{:T(128)}, ...), condition=%wide.region_1.2_spmd, body=%wide.region_0.1_spmd.sunk | while | flops 262157 | bytes 1573159 | solution.py:19
  156.5 1.2 bitcast_add_fusion.4
  157.8 1.2 bitcast_add_fusion.4
  162.7 1.2 bitcast_add_fusion.4
  166.4 1.2 bitcast_add_fusion.4
  167.7 1.2 bitcast_add_fusion.4
  170.1 1.2 bitcast_add_fusion.4
  171.4 1.2 bitcast_add_fusion.4
  172.6 1.2 bitcast_add_fusion.4
  178.8 1.2 bitcast_add_fusion.4
  181.3 1.2 bitcast_add_fusion.4
  182.6 1.2 bitcast_add_fusion.4
  183.8 1.2 bitcast_add_fusion.4
  186.3 1.2 bitcast_add_fusion.4
  187.5 1.2 bitcast_add_fusion.4
  188.8 1.2 bitcast_add_fusion.4
  197.5 2.8 fusion.9
  200.3 1.7 fusion.7
  202.0 5.2 %multiply_reduce_fusion = (f32[2,256,8]{1,2,0:T(8,128)S(1)}, f32[2,256,8,128]{1,3,2,0:T(8,128)}) fusion(f32[1,256,8,128]{1,3,2,0:T(8,128)} %fusion.7, f32[1,256,8,128]{1,3,2,0:T(8,128)} %fusion.9, bf16[2,256,8,128]{3,2,1,0:T(8,128)(2,1)S(1)} %bitcast.54, bf16[2,256,8,128]{1,3,2,0:T(8,128)(2,1)S(1)} %copy.27, f32[8,256,256]{2,1,0:T(8,128)} %exponential_select_fusion, ...), kind=kOutput, calls=%fused_computation.8 | convolution fusion | flops 541061120 | bytes 9453568 | tf_op jit(solution)/shard_map/nhij,njhd->nihd/dot_general | solution.py:67
  207.2 1.8 broadcast_multiply_fusion
  209.0 1.9 copy.35
  210.9 35.2 %all-gather.6.cloned.1.call-done = bf16[1024,6144]{0,1:T(8,128)(2,1)} async-done(((bf16[1024,96]{0,1:T(8,128)(2,1)}), bf16[1024,6144]{0,1:T(8,128)(2,1)}) %all-gather.6.cloned.1.call-update) | async-done | bytes 12582928 | tf_op jit(solution)/shard_map/all_gather | solution.py:86
  246.1 12.3 %convolution_convert_fusion = bf16[512,6144]{1,0:T(8,128)(2,1)} fusion(bf16[1024,6144]{0,1:T(8,128)(2,1)} %all-gather.6.cloned.1.call-done, f32[64,8,8,128]{3,2,1,0:T(8,128)} %bitcast.58, bf16[512,1024]{1,0:T(8,128)(2,1)S(1)} %copy-done.8, f32[1024]{0:T(1024)S(1)} %copy-done.9), kind=kOutput, calls=%fused_computation.2 | convolution fusion | flops 6449266688 | bytes 22024192 | tf_op jit(solution)/shard_map/dot_general | solution.py:84
  258.4 66.5 %reduce-scatter.2.cloned.1.call-done = bf16[512,1536]{1,0:T(8,128)(2,1)} async-done(((bf16[512,6144]{1,0:T(8,128)(2,1)}), bf16[512,1536]{1,0:T(8,128)(2,1)}) %reduce-scatter.2.cloned.1.call-update) | async-done | bytes 1572880 | tf_op jit(solution)/shard_map/reduce_scatter | solution.py:89
  (94 shorter events, 27.8 us)
Async XLA Ops:
  6.5 149.8 %all-gather.4.cloned.1.call-start = ((), (), s32[]{:S(2)}) async-start(), calls=%async_computation.1 | async-start | bytes 34078720 | tf_op jit(solution)/shard_map/all_gather | solution.py:11
  6.5 2.3 copy-start.6
  8.1 1.0 copy-start.10
  8.1 2.2 copy-start.7
  10.6 130.3 %copy-start.2 = (bf16[512,1024]{1,0:T(8,128)(2,1)S(1)}, bf16[512,1024]{1,0:T(8,128)(2,1)}, u32[]{:S(2)}) copy-start(bf16[512,1024]{1,0:T(8,128)(2,1)} %param.10) | copy-start | bytes 3145732
  12.0 1.0 copy-start
  13.9 232.2 %all-gather.6.cloned.1.call-start = ((), (), s32[]{:S(2)}) async-start(), calls=%async_computation.2 | async-start | bytes 12779520 | tf_op jit(solution)/shard_map/all_gather | solution.py:86
  14.6 310.2 %reduce-scatter.2.cloned.1.call-start = ((), (), s32[]{:S(2)}) async-start(), calls=%async_computation.3 | async-start | bytes 7864320 | tf_op jit(solution)/shard_map/reduce_scatter | solution.py:89
  156.4 41.0 %copy-start.4 = (bf16[256,1024]{0,1:T(8,128)(2,1)S(1)}, bf16[256,1024]{0,1:T(8,128)(2,1)}, u32[]{:S(2)}) copy-start(bf16[256,1024]{0,1:T(8,128)(2,1)} %copy.40) | copy-start | bytes 1572868
  197.4 2.9 copy-start.1
  197.4 2.9 copy-start.3
  197.4 2.9 copy-start.5
  208.9 37.1 %copy-start.8 = (bf16[512,1024]{1,0:T(8,128)(2,1)S(1)}, bf16[512,1024]{1,0:T(8,128)(2,1)}, u32[]{:S(2)}) copy-start(bf16[512,1024]{1,0:T(8,128)(2,1)} %param.13) | copy-start | bytes 3145732
  209.0 37.1 %copy-start.9 = (f32[1024]{0:T(1024)S(1)}, f32[1024]{0:T(1024)}, u32[]{:S(2)}) copy-start(f32[1024]{0:T(1024)} %param.16) | copy-start | bytes 12292
Sparse Core Ops, SparseCore 0:
  14.0 142.3 all-gather.3
  159.1 86.9 all-gather.5
  258.5 66.2 reduce-scatter.1
where the time goes:
time: 337 us; the launch traced here: 331 us
  blocking collectives  126 us (37%)
  waiting for transfers between devices  109 us (32%)
  other arithmetic  44.7 us (13%)
  matrix products  23.4 us (7%)
  between operations  14 us (4%)
  local copies, waits for them, and re-layouts  12.7 us (4%)
    unnamed x1, blocking collectives  126 us
    reduce_scatter x1, waiting for transfers between devices, body(): lax.psum_scatter(terms.astype(jnp.bfloat16), 'head', scatter_dimension=1,...  66.5 us
    add x33, other arithmetic, combine(): later[0][:, None, None] * earlier[1] + later[1]  39.4 us
    all_gather x1, waiting for transfers between devices, body(): lax.all_gather(out_weight, 'ctx', axis=1, tiled=True)  35.2 us
    dot_general x1, matrix products, body(): jnp.dot(hidden, lax.all_gather(out_weight, 'ctx', axis=1, tiled=True), pr...  12.3 us
    unnamed x29, local copies, waits for them, and re-layouts  8.98 us
    all_gather x1, waiting for transfers between devices, entering(): gathered = jax.tree.map(lambda a: lax.all_gather(a, axis), part)  7.02 us
  transfers between devices with their start and end apart: 3, of which 3 were waited for; matrix products, arithmetic and copies ran while one was open for 19% of the time, Pallas kernels for 0%

commit v1 on v0

v1 whole, which is shorter than its diff:
```python
import jax
import jax.numpy as jnp
from jax import lax
from jax.sharding import PartitionSpec as P
from jax.experimental import pallas as pl
from jax.experimental.pallas import tpu as pltpu

MESH = pl.DeviceIdType.MESH
F32 = jnp.float32
BF16 = jnp.bfloat16
HD = 128
BLK = 256
ROWS = 512
NH = 8


def dot(a, b, ca=1, cb=0):
    return lax.dot_general(a, b, (((ca,), (cb,)), ((), ())), preferred_element_type=F32)


def kernel(
    rate, gain, init, q_hbm, k_hbm, v_hbm, g_hbm, hid,
    q, k, v, g, u, gs, c0, loc, rx1, exc, tx2, rx2, tx3, rx3,
    lsem, s1, r1, s2, r2, s3, r3,
):
    c = lax.axis_index("ctx")
    y = lax.axis_index("head")
    z = c // 8
    me = c % 8

    barrier = pltpu.get_barrier_semaphore()
    for d in range(1, 8):
        pl.semaphore_signal(
            barrier, inc=1, device_id=(z * 8 + (me + d) % 8, y), device_id_type=MESH
        )
        pl.semaphore_signal(
            barrier, inc=1, device_id=(((z + d) % 8) * 8 + me, y), device_id_type=MESH
        )
    loads = [
        pltpu.make_async_copy(a, b, lsem.at[i])
        for i, (a, b) in enumerate(((k_hbm, k), (v_hbm, v), (q_hbm, q), (g_hbm, g)))
    ]
    for cp in loads:
        cp.start()
    loads[0].wait()
    loads[1].wait()

    col = lax.broadcasted_iota(jnp.int32, (BLK, HD), 0).astype(F32)

    for h in range(NH):
        r = rate[h]
        hs = slice(h * HD, (h + 1) * HD)
        kw = jnp.exp(-r * (BLK - 1.0 - col))
        k0 = (k[0:BLK, hs].astype(F32) * kw).astype(BF16)
        k1 = (k[BLK:ROWS, hs].astype(F32) * kw).astype(BF16)
        a0 = dot(k0, v[0:BLK, hs], 0, 0)
        a1 = dot(k1, v[BLK:ROWS, hs], 0, 0)
        c0[h] = a0.astype(BF16)
        loc[h] = (jnp.exp(jnp.full((1, HD), -r * BLK)) * a0 + a1).astype(BF16)

    rx1[me] = loc[me]
    pl.semaphore_wait(barrier, 14)
    sends = []
    for d in range(1, 8):
        to = (me + d) % 8
        cp = pltpu.make_async_remote_copy(
            src_ref=loc.at[to], dst_ref=rx1.at[me], send_sem=s1.at[d - 1],
            recv_sem=r1.at[me], device_id=(z * 8 + to, y), device_id_type=MESH,
        )
        cp.start()
        sends.append(cp)

    loads[2].wait()
    loads[3].wait()
    ii = lax.broadcasted_iota(jnp.int32, (BLK, BLK), 0)
    jj = lax.broadcasted_iota(jnp.int32, (BLK, BLK), 1)
    off = (ii - jj).astype(F32)

    def intra(h):
        r = rate[h]
        hs = slice(h * HD, (h + 1) * HD)
        decay = jnp.where(off >= 0.0, jnp.exp(-r * jnp.maximum(off, 0.0)), 0.0)
        for b in range(2):
            rs = slice(b * BLK, (b + 1) * BLK)
            w = (dot(q[rs, hs], k[rs, hs], 1, 1) * decay).astype(BF16)
            o = dot(w, v[rs, hs])
            if b == 1:
                o = o + jnp.exp(-r * (col + 1.0)) * dot(q[rs, hs], c0[h])
            u[rs, hs] = o
        gs[:, hs] = jax.nn.sigmoid(g[:, hs].astype(F32)) * gain[:, hs]

    for h in range(3):
        intra(h)

    for d in range(1, 8):
        p = (me + 8 - d) % 8
        pltpu.make_async_remote_copy(
            src_ref=loc.at[0], dst_ref=rx1.at[p], send_sem=s1.at[0],
            recv_sem=r1.at[p], device_id=(z * 8 + p, y), device_id_type=MESH,
        ).wait_recv()
    rm = rate[me]
    d512 = jnp.exp(jnp.full((1, HD), -rm * 512.0))
    e = jnp.zeros((HD, HD), F32)
    for p in range(8):
        exc[p] = e
        e = d512 * e + rx1[p].astype(F32)
    tx2[...] = e.astype(BF16)
    for d in range(1, 8):
        @pl.when(z + d < 8)
        def _():
            pltpu.make_async_remote_copy(
                src_ref=tx2, dst_ref=rx2.at[z], send_sem=s2.at[d - 1],
                recv_sem=r2.at[z], device_id=((z + d) % 8 * 8 + me, y), device_id_type=MESH,
            ).start()

    for h in range(3, NH):
        intra(h)

    tx3[...] = init[me]
    for i in range(7):
        @pl.when(i < z)
        def _():
            pltpu.make_async_remote_copy(
                src_ref=tx2, dst_ref=rx2.at[i], send_sem=s2.at[0],
                recv_sem=r2.at[i], device_id=(i * 8 + me, y), device_id_type=MESH,
            ).wait_recv()
            tx3[...] = jnp.exp(jnp.full((1, HD), -rm * 4096.0)) * tx3[...] + rx2[i].astype(F32)
    base = tx3[...]
    for p in range(8):
        rx1[p] = (jnp.exp(jnp.full((1, HD), -rm * (512.0 * p))) * base + exc[p]).astype(BF16)
    rx3[me] = rx1[me]
    for d in range(1, 8):
        to = (me + d) % 8
        cp = pltpu.make_async_remote_copy(
            src_ref=rx1.at[to], dst_ref=rx3.at[me], send_sem=s3.at[d - 1],
            recv_sem=r3.at[me], device_id=(z * 8 + to, y), device_id_type=MESH,
        )
        cp.start()
        sends.append(cp)

    row = lax.broadcasted_iota(jnp.int32, (ROWS, HD), 0).astype(F32)
    for h in range(NH):
        @pl.when(h != me)
        def _():
            pltpu.make_async_remote_copy(
                src_ref=rx1.at[0], dst_ref=rx3.at[h], send_sem=s3.at[0],
                recv_sem=r3.at[h], device_id=(z * 8 + h, y), device_id_type=MESH,
            ).wait_recv()
        hs = slice(h * HD, (h + 1) * HD)
        at = u[:, hs] + jnp.exp(-rate[h] * (row + 1.0)) * dot(q[:, hs], rx3[h])
        scale = lax.rsqrt(jnp.mean(at * at, axis=-1, keepdims=True) + 1e-06)
        hid[:, hs] = (at * scale * gs[:, hs]).astype(BF16)

    for cp in sends:
        cp.wait_send()
    for d in range(1, 8):
        @pl.when(z + d < 8)
        def _():
            pltpu.make_async_remote_copy(
                src_ref=tx2, dst_ref=rx2.at[z], send_sem=s2.at[d - 1],
                recv_sem=r2.at[z], device_id=((z + d) % 8 * 8 + me, y), device_id_type=MESH,
            ).wait_send()


def body(
    query_rows, key_rows, value_rows, gate_rows, init_state, decay_rate, norm_gain, out_weight
):
    vm = pl.BlockSpec(memory_space=pltpu.VMEM)
    anyspace = pl.BlockSpec(memory_space=pl.ANY)
    dma = pltpu.SemaphoreType.DMA
    hidden = pl.pallas_call(
        kernel,
        out_shape=jax.ShapeDtypeStruct((ROWS, NH * HD), BF16),
        in_specs=[pl.BlockSpec(memory_space=pltpu.SMEM), vm, vm] + [anyspace] * 4,
        out_specs=vm,
        scratch_shapes=[
            pltpu.VMEM((ROWS, NH * HD), BF16),
            pltpu.VMEM((ROWS, NH * HD), BF16),
            pltpu.VMEM((ROWS, NH * HD), BF16),
            pltpu.VMEM((ROWS, NH * HD), BF16),
            pltpu.VMEM((ROWS, NH * HD), F32),
            pltpu.VMEM((ROWS, NH * HD), F32),
            pltpu.VMEM((NH, HD, HD), BF16),
            pltpu.VMEM((NH, HD, HD), BF16),
            pltpu.VMEM((8, HD, HD), BF16),
            pltpu.VMEM((8, HD, HD), F32),
            pltpu.VMEM((HD, HD), BF16),
            pltpu.VMEM((8, HD, HD), BF16),
            pltpu.VMEM((HD, HD), F32),
            pltpu.VMEM((NH, HD, HD), BF16),
            dma((4,)), dma((7,)), dma((8,)), dma((7,)), dma((8,)), dma((7,)), dma((8,)),
        ],
        compiler_params=pltpu.CompilerParams(
            collective_id=0, has_side_effects=True, vmem_limit_bytes=40 * 2**20
        ),
        cost_estimate=pl.CostEstimate(flops=10**9, bytes_accessed=6 * 2**20, transcendentals=10**6),
    )(decay_rate, norm_gain[None, :], init_state, query_rows, key_rows, value_rows, gate_rows)
    terms = jnp.dot(
        hidden,
        lax.all_gather(out_weight, "ctx", axis=1, tiled=True),
        preferred_element_type=F32,
    )
    return lax.psum_scatter(terms.astype(BF16), "head", scatter_dimension=1, tiled=True)


def solution(mesh):
    return jax.shard_map(
        body,
        mesh=mesh,
        in_specs=(
            P("ctx", "head"),
            P("ctx", "head"),
            P("ctx", "head"),
            P("ctx", "head"),
            P("head", None, None),
            P("head"),
            P("head"),
            P("head", "ctx"),
        ),
        out_specs=P("ctx", "head"),
        check_vma=False,
    )
```

time: 337 us -> 194 us (0.58)
  blocking collectives: 126 us -> 0 us
  other arithmetic: 44.7 us -> 0 us
  Pallas kernels: 0 us -> 26.6 us
  waiting for transfers between devices: 109 us -> 125 us
  local copies, waits for them, and re-layouts: 12.7 us -> 7.27 us
  matrix products: 23.4 us -> 18.8 us
    unnamed x1 -> x0, blocking collectives: 126 us -> none
    add x35 -> x0, other arithmetic: 40.3 us -> none  [the longest x33 39.4 us: combine(): later[0][:, None, None] * earlier[1] + later[1]]
    pallas_call x0 -> x1, Pallas kernels: none -> 26.6 us  [body(): pl.pallas_call(kernel, out_shape=jax.ShapeDtypeStruct((ROWS, NH * HD), BF...]
    all_gather x1, waiting for transfers between devices: 35.2 us -> 58.2 us  [body(): lax.all_gather(out_weight, 'ctx', axis=1, tiled=True)]
    dot_general x4 -> x0, matrix products: 11.1 us -> none  [the longest x1 5.17 us: body(): jnp.einsum('nhij,njhd->nihd', weights_bf, value_blocks, preferred_element...]
    all_gather x1 -> x0, waiting for transfers between devices: 7.02 us -> none  [entering(): gathered = jax.tree.map(lambda a: lax.all_gather(a, axis), part)]
    dot_general x1, matrix products: 12.3 us -> 18.8 us  [body(): jnp.dot(hidden, lax.all_gather(out_weight, 'ctx', axis=1, tiled=True), pr...]
    unnamed x29 -> x14, local copies, waits for them, and re-layouts: 8.98 us -> 7.27 us
  transfers between devices with their start and end apart: 3 -> 2, of which waited for: 3 -> 2; matrix products, arithmetic and copies ran while one was open for 19% -> 0% of each run, Pallas kernels for 0% -> 14%
where the time goes in v1:
time: 194 us; the launch traced here: 191 us
  waiting for transfers between devices  125 us (64%)
  Pallas kernels  26.6 us (14%)
  matrix products  18.8 us (10%)
  between operations  13.4 us (7%)
  local copies, waits for them, and re-layouts  7.27 us (4%)
    reduce_scatter x1, waiting for transfers between devices, body(): lax.psum_scatter(terms.astype(BF16), 'head', scatter_dimension=1, tiled=T...  66.1 us
    all_gather x1, waiting for transfers between devices, body(): lax.all_gather(out_weight, 'ctx', axis=1, tiled=True)  58.2 us
    pallas_call x1, Pallas kernels, body(): pl.pallas_call(kernel, out_shape=jax.ShapeDtypeStruct((ROWS, NH * HD), BF...  26.6 us
    dot_general x1, matrix products, body(): jnp.dot(hidden, lax.all_gather(out_weight, 'ctx', axis=1, tiled=True), pr...  18.8 us
    unnamed x14, local copies, waits for them, and re-layouts  7.27 us
  transfers between devices with their start and end apart: 2, of which 2 were waited for; matrix products, arithmetic and copies ran while one was open for 0% of the time, Pallas kernels for 14%

profile of v1, /device:TPU:129, one launch (start us, length us, event | category | flops | bytes accessed | tf_op | source)
XLA Modules:
  0.0 191.2 jit_solution(1464571170264149289)
XLA Ops:
  6.5 0.0 all-gather.2.cloned.1.call-start
  6.5 0.7 all-gather.2.cloned.1.call-update
  7.3 0.0 reduce-scatter.2.cloned.1.call-start
  7.3 0.0 copy-start
  7.3 1.2 copy-done
  8.5 0.0 copy-start.1
  8.5 1.2 copy-done.1
  9.8 0.0 copy-start.2
  9.8 1.2 copy-done.2
  11.0 0.0 copy-start.3
  11.0 1.2 copy-done.3
  12.2 0.0 copy-start.4
  12.2 1.0 copy-done.4
  13.2 0.0 copy-start.5
  13.2 0.7 copy-done.5
  13.9 0.0 copy-start.6
  13.9 0.7 copy-done.6
  14.6 26.6 %shard_map.82 = bf16[512,1024]{1,0:T(8,128)(2,1)S(1)} custom-call(f32[8]{0:T(128)S(1)} %copy-done.6, f32[1,1024]{1,0:T(1,128)S(1)} %bitcast.3, f32[8,128,128]{2,1,0:T(8,128)S(1)} %copy-done.4, bf16[512,1024]{1,0:T(8,128)(2,1)S(1)} %copy-done, bf16[512,1024]{1,0:T(8,128)(2,1)S(1)} %copy-done.1, bf16[512,1024]{1,0:T(8,128)(2,1)S(1)} %copy-done.2, ...), custom_call_target="tpu_custom_call" | custom-call | flops 1000000000 | bytes 6291456 | tf_op jit(solution)/shard_map/pallas_call | solution.py:171
  41.2 58.2 %all-gather.2.cloned.1.call-done = bf16[1024,6144]{0,1:T(8,128)(2,1)} async-done(((bf16[1024,96]{0,1:T(8,128)(2,1)}), bf16[1024,6144]{0,1:T(8,128)(2,1)}) %all-gather.2.cloned.1.call-update) | async-done | bytes 12582928 | tf_op jit(solution)/shard_map/all_gather | solution.py:200
  99.5 18.8 %convolution_convert_fusion = bf16[512,6144]{1,0:T(8,128)(2,1)} fusion(bf16[512,1024]{1,0:T(8,128)(2,1)S(1)} %shard_map.82, bf16[1024,6144]{0,1:T(8,128)(2,1)} %all-gather.2.cloned.1.call-done), kind=kOutput, calls=%fused_computation | convolution fusion | flops 6445596672 | bytes 19922944 | tf_op jit(solution)/shard_map/dot_general | solution.py:198
  118.2 0.0 reduce-scatter.2.cloned.1.call-update
  118.3 66.1 %reduce-scatter.2.cloned.1.call-done = bf16[512,1536]{1,0:T(8,128)(2,1)} async-done(((bf16[512,6144]{1,0:T(8,128)(2,1)}), bf16[512,1536]{1,0:T(8,128)(2,1)}) %reduce-scatter.2.cloned.1.call-update) | async-done | bytes 1572880 | tf_op jit(solution)/shard_map/reduce_scatter | solution.py:203
Async XLA Ops:
  6.5 92.9 %all-gather.2.cloned.1.call-start = ((), (), s32[]{:S(2)}) async-start(), calls=%async_computation.1 | async-start | bytes 12779520 | tf_op jit(solution)/shard_map/all_gather | solution.py:200
  7.3 177.1 %reduce-scatter.2.cloned.1.call-start = ((), (), s32[]{:S(2)}) async-start(), calls=%async_computation.2 | async-start | bytes 7864320 | tf_op jit(solution)/shard_map/reduce_scatter | solution.py:203
  7.3 1.2 copy-start
  8.5 1.2 copy-start.1
  9.8 1.2 copy-start.2
  11.0 1.2 copy-start.3
  12.2 1.0 copy-start.4
  13.2 0.7 copy-start.5
  13.9 0.7 copy-start.6
Sparse Core Ops, SparseCore 0:
  10.1 89.2 all-gather.1
  118.4 65.9 reduce-scatter.1

commit v2 on v1

v2 whole, which is shorter than its diff:
```python
import jax
import jax.numpy as jnp
from jax import lax
from jax.sharding import PartitionSpec as P
from jax.experimental import pallas as pl
from jax.experimental.pallas import tpu as pltpu

MESH = pl.DeviceIdType.MESH
F32 = jnp.float32
BF16 = jnp.bfloat16
HD = 128
BLK = 256
ROWS = 512
NH = 8


def dot(a, b, ca=1, cb=0):
    return lax.dot_general(a, b, (((ca,), (cb,)), ((), ())), preferred_element_type=F32)

ORD = (0, 1, 3, 2)


def kernel(
    rate, gain, init, q_hbm, k_hbm, v_hbm, g_hbm, w_hbm, out,
    q, k, v, g, u, gs, c0, loc, rx1, exc, tx2, rx2, tx3, rx3, zb, wt, hidg, acc,
    lsem, s1, r1, s2, r2, s3, r3,
    su, ru, sd, rd, sy, ry, sxu, rxu, sxd, rxd, srl, rrl, szp, rzp, s2d, r2d,
    shu, rhu, shd, rhd, shr, rhr,
):
    c = lax.axis_index("ctx")
    y = lax.axis_index("head")
    z = c // 8
    me = c % 8
    x = me // 2
    core = me % 2
    par = z % 2
    xup, xdn, xop = (x + 1) % 4, (x + 3) % 4, (x + 2) % 4

    def dev(zz, xx, yy, cc=core):
        return (zz * 8 + xx * 2 + cc, yy)

    def rcopy(src, dst, ss, rs, to):
        return pltpu.make_async_remote_copy(
            src_ref=src, dst_ref=dst, send_sem=ss, recv_sem=rs, device_id=to, device_id_type=MESH
        )

    barrier = pltpu.get_barrier_semaphore()
    for d in range(1, 8):
        pl.semaphore_signal(
            barrier, inc=1, device_id=(z * 8 + (me + d) % 8, y), device_id_type=MESH
        )
        pl.semaphore_signal(
            barrier, inc=1, device_id=(((z + d) % 8) * 8 + me, y), device_id_type=MESH
        )
    for d in range(1, 4):
        pl.semaphore_signal(barrier, inc=1, device_id=(c, (y + d) % 4), device_id_type=MESH)
    loads = [
        pltpu.make_async_copy(a, b, lsem.at[i])
        for i, (a, b) in enumerate(
            (
                (k_hbm, k), (v_hbm, v), (w_hbm, zb.at[z]), (q_hbm, q), (g_hbm, g),
                (init.at[me], tx3),
            )
        )
    ]
    for cp in loads:
        cp.start()

    def z_send(s):
        if s == 0:
            rcopy(zb.at[z], zb.at[z], su.at[0], ru.at[0], dev((z + 1) % 8, x, y)).start()
            rcopy(zb.at[z], zb.at[z], sd.at[0], rd.at[0], dev((z + 7) % 8, x, y)).start()
            return
        lo, hi = (z + 8 - s) % 8, (z + s) % 8
        for part in (0, 1):
            zs = lo if part == 0 else hi
            sems = (su, ru) if part == 0 else (sd, rd)
            to = dev((z + 1) % 8 if part == 0 else (z + 7) % 8, x, y)
            if s == 4:
                rows = pl.ds(48 * part, 48)
                rcopy(zb.at[zs, rows], zb.at[zs, rows], sems[0].at[3], sems[1].at[3], to).wait_recv()
            else:
                rcopy(zb.at[zs], zb.at[zs], sems[0].at[s - 1], sems[1].at[s - 1], to).wait_recv()
                if s == 3:
                    rows = pl.ds(48 * part, 48)
                    rcopy(zb.at[zs, rows], zb.at[zs, rows], sems[0].at[3], sems[1].at[3], to).start()
                else:
                    rcopy(zb.at[zs], zb.at[zs], sems[0].at[s], sems[1].at[s], to).start()

    def y_copy(zs):
        j = zs % 2
        return rcopy(zb.at[zs], wt.at[y, x, j, core], sy.at[zs], ry.at[y, j], dev(z, x, zs // 2))

    def y_send(zs):
        j = zs % 2

        @pl.when(zs // 2 == y)
        def _():
            pltpu.make_async_copy(zb.at[zs], wt.at[y, x, j, core], ry.at[y, j]).start()

        @pl.when(zs // 2 != y)
        def _():
            y_copy(zs).start()

    def z_event(s):
        z_send(s)
        y_send((z + 8 - s) % 8)
        if s in (1, 2, 3):
            y_send((z + s) % 8)

    def dist(j):
        d = (2 * y + j + 8 - z) % 8
        return jnp.minimum(d, 8 - d)

    first = jnp.where(dist(0) < dist(1), 0, 1)

    def piece(i, quarter, j):
        return wt.at[(y + ORD[i]) % 4, quarter, j, core]

    def up_copy(i, j):
        p = piece(i, x, j)
        return rcopy(p, p, sxu.at[j, i], rxu.at[j, i], dev(z, xup, y))

    def dn_copy(i, j):
        p = piece(i, x, j)
        return rcopy(p, p, sxd.at[j, i], rxd.at[j, i], dev(z, xdn, y))

    def pair_copy(which, i, j):
        quarter = (x, xdn, xup, xop)[which]
        p = wt.at[(y + order_at(i)) % 4, quarter, j, core]
        return rcopy(p, p, s2d.at[which, j, i], r2d.at[which, j, i], dev(z, x, y, 1 - core))

    def order_at(i):
        if isinstance(i, int):
            return ORD[i]
        return jnp.where(i == 3, 2, jnp.where(i == 2, 3, i))

    def x_send(j):
        for i in range(4):
            yy = (y + ORD[i]) % 4
            rcopy(
                zb.at[0], wt.at[yy, x, j, core], sy.at[0], ry.at[yy, j], dev(z, x, (y + 1) % 4)
            ).wait_recv()
            up_copy(i, j).start()
            dn_copy(i, j).start()
            pair_copy(0, i, j).start()

    def x_stage(s):
        for j in range(2):
            @pl.when(dist(j) == s)
            def _():
                x_send(j)

    def relay_copy(m, j):
        i = 2 * par + m
        quarter, to = (xdn, xup) if m == 0 else (xup, xdn)
        p = wt.at[(y + order_at(i)) % 4, quarter, j, core]
        return rcopy(p, p, srl.at[j, m], rrl.at[j, m], dev(z, to, y))

    def x_event(n):
        j = first if n < 4 else 1 - first
        i = n % 4
        up_copy(i, j).wait_recv()
        pair_copy(1, i, j).start()
        if i % 2 == 0:
            @pl.when(par == i // 2)
            def _():
                relay_copy(0, j).start()
        dn_copy(i, j).wait_recv()
        pair_copy(2, i, j).start()
        if i % 2 == 1:
            @pl.when(par == i // 2)
            def _():
                relay_copy(1, j).start()

    def zpair_copy(m, j, mine):
        i = 2 * par + m if mine else 2 * (1 - par) + m
        p = wt.at[(y + order_at(i)) % 4, xop, j, core]
        return rcopy(p, p, szp.at[j, m], rzp.at[j, m], dev(z + 1 - 2 * par, x, y))

    def opposite_event(n):
        j = first if n < 2 else 1 - first
        m = n % 2
        p = wt.at[(y + order_at(2 * par + m)) % 4, xop, j, core]
        rcopy(p, p, srl.at[j, m], rrl.at[j, m], dev(z, xup, y)).wait_recv()
        zpair_copy(m, j, True).start()
        pair_copy(3, 2 * par + m, j).start()

    def zpair_event(n):
        j = first if n < 2 else 1 - first
        m = n % 2
        zpair_copy(m, j, False).wait_recv()
        pair_copy(3, 2 * (1 - par) + m, j).start()

    def pair_wait(which):
        for j in range(2):
            for i in range(4):
                pair_copy_in(which, i, j).wait_recv()

    def pair_copy_in(which, i, j):
        quarter = (x, xdn, xup, xop)[which]
        p = wt.at[(y + ORD[i]) % 4, quarter, j, 1 - core]
        return rcopy(p, p, s2d.at[which, j, i], r2d.at[which, j, i], dev(z, x, y, 1 - core))

    yup, ydn, yop = (y + 1) % 4, (y + 3) % 4, (y + 2) % 4

    def chunk(who, n):
        return hidg.at[who, :, pl.ds(n * 256, 256)]

    def h_up(n):
        return rcopy(chunk(y, n), chunk(y, n), shu.at[n], rhu.at[n], dev(z, x, yup))

    def h_dn(n):
        return rcopy(chunk(y, n), chunk(y, n), shd.at[n], rhd.at[n], dev(z, x, ydn))

    def h_relay(n):
        who, to = (ydn, yup) if n < 2 else (yup, ydn)
        return rcopy(chunk(who, n), chunk(who, n), shr.at[n], rhr.at[n], dev(z, x, to))

    def h_event(n):
        h_up(n).wait_recv()
        if n < 2:
            h_relay(n).start()
        h_dn(n).wait_recv()
        if n >= 2:
            h_relay(n).start()

    def unit(who, quarter, start=False):
        t = dot(hidg[who], wt[who, quarter].reshape(384, 1024), 1, 1)
        acc[quarter] = t if start else acc[quarter] + t

    loads[0].wait()
    loads[1].wait()
    col = lax.broadcasted_iota(jnp.int32, (BLK, HD), 0).astype(F32)
    for h in range(NH):
        r = rate[h]
        hs = slice(h * HD, (h + 1) * HD)
        kw = jnp.exp(-r * (BLK - 1.0 - col))
        k0 = (k[0:BLK, hs].astype(F32) * kw).astype(BF16)
        k1 = (k[BLK:ROWS, hs].astype(F32) * kw).astype(BF16)
        a0 = dot(k0, v[0:BLK, hs], 0, 0)
        a1 = dot(k1, v[BLK:ROWS, hs], 0, 0)
        c0[h] = a0.astype(BF16)
        loc[h] = (jnp.exp(jnp.full((1, HD), -r * BLK)) * a0 + a1).astype(BF16)

    rx1[me] = loc[me]
    loads[2].wait()
    pl.semaphore_wait(barrier, 17)
    sends = []
    for d in range(1, 8):
        to = (me + d) % 8
        cp = rcopy(loc.at[to], rx1.at[me], s1.at[d - 1], r1.at[me], (z * 8 + to, y))
        cp.start()
        sends.append(cp)
    z_send(0)
    y_send(z)

    loads[3].wait()
    loads[4].wait()
    loads[5].wait()
    ii = lax.broadcasted_iota(jnp.int32, (BLK, BLK), 0)
    jj = lax.broadcasted_iota(jnp.int32, (BLK, BLK), 1)
    off = (ii - jj).astype(F32)

    def intra(h):
        r = rate[h]
        hs = slice(h * HD, (h + 1) * HD)
        decay = jnp.where(off >= 0.0, jnp.exp(-r * jnp.maximum(off, 0.0)), 0.0)
        for b in range(2):
            rs = slice(b * BLK, (b + 1) * BLK)
            w = (dot(q[rs, hs], k[rs, hs], 1, 1) * decay).astype(BF16)
            o = dot(w, v[rs, hs])
            if b == 1:
                o = o + jnp.exp(-r * (col + 1.0)) * dot(q[rs, hs], c0[h])
            u[rs, hs] = o
        gs[:, hs] = jax.nn.sigmoid(g[:, hs].astype(F32)) * gain[:, hs]

    for h in range(3):
        intra(h)

    for d in range(1, 8):
        p = (me + 8 - d) % 8
        rcopy(loc.at[0], rx1.at[p], s1.at[0], r1.at[p], (z * 8 + p, y)).wait_recv()
    rm = rate[me]
    d512 = jnp.exp(jnp.full((1, HD), -rm * 512.0))
    e = jnp.zeros((HD, HD), F32)
    for p in range(8):
        exc[p] = e
        e = d512 * e + rx1[p].astype(F32)
    tx2[...] = e.astype(BF16)

    def z_state(d):
        return rcopy(tx2, rx2.at[z], s2.at[d - 1], r2.at[z], ((z + d) % 8 * 8 + me, y))

    for d in range(1, 8):
        @pl.when(z + d < 8)
        def _():
            z_state(d).start()

    z_event(1)
    for h in range(3, 6):
        intra(h)
    z_event(2)
    x_stage(0)
    x_stage(1)
    for h in range(6, NH):
        intra(h)

    for i in range(7):
        @pl.when(i < z)
        def _():
            rcopy(tx2, rx2.at[i], s2.at[0], r2.at[i], (i * 8 + me, y)).wait_recv()
            tx3[...] = jnp.exp(jnp.full((1, HD), -rm * 4096.0)) * tx3[...] + rx2[i].astype(F32)
    base = tx3[...]
    for p in range(8):
        rx1[p] = (jnp.exp(jnp.full((1, HD), -rm * (512.0 * p))) * base + exc[p]).astype(BF16)
    rx3[me] = rx1[me]
    for d in range(1, 8):
        to = (me + d) % 8
        cp = rcopy(rx1.at[to], rx3.at[me], s3.at[d - 1], r3.at[me], (z * 8 + to, y))
        cp.start()
        sends.append(cp)

    z_event(3)
    x_stage(2)

    row = lax.broadcasted_iota(jnp.int32, (ROWS, HD), 0).astype(F32)
    for h in range(NH):
        @pl.when(h != me)
        def _():
            rcopy(rx1.at[0], rx3.at[h], s3.at[0], r3.at[h], (z * 8 + h, y)).wait_recv()
        hs = slice(h * HD, (h + 1) * HD)
        at = u[:, hs] + jnp.exp(-rate[h] * (row + 1.0)) * dot(q[:, hs], rx3[h])
        scale = lax.rsqrt(jnp.mean(at * at, axis=-1, keepdims=True) + 1e-06)
        hidg[y, :, hs] = (at * scale * gs[:, hs]).astype(BF16)
        if h % 2 == 1:
            h_up(h // 2).start()
            h_dn(h // 2).start()

    z_event(4)
    x_stage(3)
    x_stage(4)

    x_event(0)
    x_event(1)
    pair_wait(0)
    unit(y, x, True)
    x_event(2)
    h_event(0)
    x_event(3)
    h_event(1)
    x_event(4)
    h_event(2)
    x_event(5)
    h_event(3)
    unit(yup, x)
    unit(ydn, x)
    x_event(6)
    x_event(7)
    pair_wait(1)
    for who in (y, ydn, yup):
        unit(who, xdn, who is y)
    pair_wait(2)
    for who in (y, ydn, yup):
        unit(who, xup, who is y)
    for n in range(4):
        opposite_event(n)
    for n in range(4):
        who, to = (yop, yup) if n < 2 else (yop, ydn)
        rcopy(chunk(yop, n), chunk(yop, n), shr.at[n], rhr.at[n], dev(z, x, to)).wait_recv()
    for quarter in (x, xdn, xup):
        unit(yop, quarter)
    for n in range(4):
        zpair_event(n)
    pair_wait(3)
    for who in (y, ydn, yup, yop):
        unit(who, xop, who is y)

    low = lax.broadcasted_iota(jnp.int32, (64, HD), 1) < 64

    def swap(t):
        return pltpu.roll(t, 64, axis=1)

    for pr in range(2):
        for rb in range(8):
            rs = slice(rb * 64, (rb + 1) * 64)
            p0, p1, p2 = (acc[2 * pr, rs, n * HD : (n + 1) * HD] for n in range(3))
            q0, q1, q2 = (acc[2 * pr + 1, rs, n * HD : (n + 1) * HD] for n in range(3))
            sp1, sp2, sq0, sq1 = swap(p1), swap(p2), swap(q0), swap(q1)
            tiles = (
                (p0, jnp.where(low, p1, sq0), jnp.where(low, sq0, sq1)),
                (jnp.where(low, sp1, sp2), jnp.where(low, sp2, q1), q2),
            )
            for j in range(2):
                for n in range(3):
                    at = j * 768 + pr * 384 + n * HD
                    out[rs, at : at + HD] = tiles[j][n].astype(BF16)

    for cp in sends:
        cp.wait_send()
    for d in range(1, 8):
        @pl.when(z + d < 8)
        def _():
            z_state(d).wait_send()
    for s in range(3):
        rcopy(zb.at[0], zb.at[0], su.at[s], ru.at[s], dev((z + 1) % 8, x, y)).wait_send()
        rcopy(zb.at[0], zb.at[0], sd.at[s], rd.at[s], dev((z + 7) % 8, x, y)).wait_send()
    half = zb.at[0, pl.ds(0, 48)]
    rcopy(half, half, su.at[3], ru.at[3], dev((z + 1) % 8, x, y)).wait_send()
    rcopy(half, half, sd.at[3], rd.at[3], dev((z + 7) % 8, x, y)).wait_send()
    for zs in range(8):
        @pl.when(zs // 2 != y)
        def _():
            y_copy(zs).wait_send()
    for j in range(2):
        for i in range(4):
            up_copy(i, j).wait_send()
            dn_copy(i, j).wait_send()
            for which in range(4):
                pair_copy(which, i, j).wait_send()
        for m in range(2):
            relay_copy(m, j).wait_send()
            zpair_copy(m, j, True).wait_send()
    for n in range(4):
        h_up(n).wait_send()
        h_dn(n).wait_send()
        h_relay(n).wait_send()


def body(
    query_rows, key_rows, value_rows, gate_rows, init_state, decay_rate, norm_gain, out_weight
):
    vm = pl.BlockSpec(memory_space=pltpu.VMEM)
    anyspace = pl.BlockSpec(memory_space=pl.ANY)
    dma = pltpu.SemaphoreType.DMA
    return pl.pallas_call(
        kernel,
        out_shape=jax.ShapeDtypeStruct((ROWS, 1536), BF16),
        in_specs=[pl.BlockSpec(memory_space=pltpu.SMEM), vm] + [anyspace] * 6,
        out_specs=vm,
        scratch_shapes=[
            pltpu.VMEM((ROWS, NH * HD), BF16),
            pltpu.VMEM((ROWS, NH * HD), BF16),
            pltpu.VMEM((ROWS, NH * HD), BF16),
            pltpu.VMEM((ROWS, NH * HD), BF16),
            pltpu.VMEM((ROWS, NH * HD), F32),
            pltpu.VMEM((ROWS, NH * HD), F32),
            pltpu.VMEM((NH, HD, HD), BF16),
            pltpu.VMEM((NH, HD, HD), BF16),
            pltpu.VMEM((8, HD, HD), BF16),
            pltpu.VMEM((8, HD, HD), F32),
            pltpu.VMEM((HD, HD), BF16),
            pltpu.VMEM((8, HD, HD), BF16),
            pltpu.VMEM((HD, HD), F32),
            pltpu.VMEM((NH, HD, HD), BF16),
            pltpu.VMEM((8, 96, 1024), BF16),
            pltpu.VMEM((4, 4, 2, 2, 96, 1024), BF16),
            pltpu.VMEM((4, ROWS, NH * HD), BF16),
            pltpu.VMEM((4, ROWS, 384), F32),
            dma((6,)), dma((7,)), dma((8,)), dma((7,)), dma((8,)), dma((7,)), dma((8,)),
            dma((4,)), dma((4,)), dma((4,)), dma((4,)), dma((8,)), dma((4, 2)),
            dma((2, 4)), dma((2, 4)), dma((2, 4)), dma((2, 4)),
            dma((2, 2)), dma((2, 2)), dma((2, 2)), dma((2, 2)),
            dma((4, 2, 4)), dma((4, 2, 4)),
            dma((4,)), dma((4,)), dma((4,)), dma((4,)), dma((4,)), dma((4,)),
        ],
        compiler_params=pltpu.CompilerParams(
            collective_id=0, has_side_effects=True, vmem_limit_bytes=60 * 2**20
        ),
        cost_estimate=pl.CostEstimate(
            flops=8 * 10**9, bytes_accessed=6 * 2**20, transcendentals=10**6
        ),
    )(
        decay_rate, norm_gain[None, :], init_state, query_rows, key_rows, value_rows, gate_rows,
        out_weight.T,
    )


def solution(mesh):
    return jax.shard_map(
        body,
        mesh=mesh,
        in_specs=(
            P("ctx", "head"),
            P("ctx", "head"),
            P("ctx", "head"),
            P("ctx", "head"),
            P("head", None, None),
            P("head"),
            P("head"),
            P("head", "ctx"),
        ),
        out_specs=P("ctx", "head"),
        check_vma=False,
    )
```

time: 194 us -> 134 us (0.69)
  waiting for transfers between devices: 125 us -> 0 us
  Pallas kernels: 26.6 us -> 130 us
  matrix products: 18.8 us -> 0 us
  between operations: 13.4 us -> 0.01 us
  local copies, waits for them, and re-layouts: 7.27 us -> 2.65 us
    pallas_call x1, Pallas kernels: 26.6 us -> 130 us  [body(): pl.pallas_call(kernel, out_shape=jax.ShapeDtypeStruct((ROWS, 1536), BF16)...]
    reduce_scatter x1 -> x0, waiting for transfers between devices: 66.1 us -> none  [body(): lax.psum_scatter(terms.astype(BF16), 'head', scatter_dimension=1, tiled=T...]
    all_gather x1 -> x0, waiting for transfers between devices: 58.2 us -> none  [body(): lax.all_gather(out_weight, 'ctx', axis=1, tiled=True)]
    dot_general x1 -> x0, matrix products: 18.8 us -> none  [body(): jnp.dot(hidden, lax.all_gather(out_weight, 'ctx', axis=1, tiled=True), pr...]
    unnamed x14 -> x1, local copies, waits for them, and re-layouts: 7.27 us -> 2.65 us
  transfers between devices with their start and end apart: 2 -> 0, of which waited for: 2 -> 0; matrix products, arithmetic and copies ran while one was open for 0% -> 0% of each run, Pallas kernels for 14% -> 0%
where the time goes in v2:
time: 134 us; the launch traced here: 132 us
  Pallas kernels  130 us (97%)
  local copies, waits for them, and re-layouts  2.65 us (2%)
    pallas_call x1, Pallas kernels, body(): pl.pallas_call(kernel, out_shape=jax.ShapeDtypeStruct((ROWS, 1536), BF16)...  130 us

profile of v2, /device:TPU:129, one launch (start us, length us, event | category | flops | bytes accessed | tf_op | source)
XLA Modules:
  0.0 132.3 jit_solution(6868434372465620775)
XLA Ops:
  0.0 129.7 %shard_map.82 = bf16[512,1536]{1,0:T(8,128)(2,1)} custom-call(f32[8]{0:T(128)} %rate.1, f32[1,1024]{1,0:T(1,128)} %bitcast.3, f32[8,128,128]{2,1,0:T(8,128)} %init.1, bf16[512,1024]{1,0:T(8,128)(2,1)} %q_hbm.1, bf16[512,1024]{1,0:T(8,128)(2,1)} %k_hbm.1, bf16[512,1024]{1,0:T(8,128)(2,1)} %v_hbm.1, bf16[512,1024]{1,0:T(8,128)(2,1)} %g_hbm.1, ...), custom_call_target="tpu_custom_call" | custom-call | flops 8000000000 | bytes 6291456 | tf_op jit(solution)/shard_map/pallas_call | solution.py:436
  129.7 2.7 %copy.10 = bf16[512,1536]{1,0:T(8,128)(2,1)} copy(bf16[512,1536]{1,0:T(8,128)(2,1)} %shard_map.82) | data formatting | bytes 3145728

commit v3 on v2

--- a/solution.py
+++ b/solution.py
@@ -24,7 +24,7 @@
     rate, gain, init, q_hbm, k_hbm, v_hbm, g_hbm, w_hbm, out,
     q, k, v, g, u, gs, c0, loc, rx1, exc, tx2, rx2, tx3, rx3, zb, wt, hidg, acc,
     lsem, s1, r1, s2, r2, s3, r3,
-    su, ru, sd, rd, sy, ry, sxu, rxu, sxd, rxd, srl, rrl, szp, rzp, s2d, r2d,
+    sz, rz, sy, ry, sx, rx, srl, rrl, szp, rzp, s2d, r2d,
     shu, rhu, shd, rhd, shr, rhr,
 ):
     c = lax.axis_index("ctx")
@@ -66,83 +66,101 @@
     for cp in loads:
         cp.start()
 
-    def z_send(s):
-        if s == 0:
-            rcopy(zb.at[z], zb.at[z], su.at[0], ru.at[0], dev((z + 1) % 8, x, y)).start()
-            rcopy(zb.at[z], zb.at[z], sd.at[0], rd.at[0], dev((z + 7) % 8, x, y)).start()
-            return
-        lo, hi = (z + 8 - s) % 8, (z + s) % 8
-        for part in (0, 1):
-            zs = lo if part == 0 else hi
-            sems = (su, ru) if part == 0 else (sd, rd)
-            to = dev((z + 1) % 8 if part == 0 else (z + 7) % 8, x, y)
-            if s == 4:
-                rows = pl.ds(48 * part, 48)
-                rcopy(zb.at[zs, rows], zb.at[zs, rows], sems[0].at[3], sems[1].at[3], to).wait_recv()
-            else:
-                rcopy(zb.at[zs], zb.at[zs], sems[0].at[s - 1], sems[1].at[s - 1], to).wait_recv()
-                if s == 3:
-                    rows = pl.ds(48 * part, 48)
-                    rcopy(zb.at[zs, rows], zb.at[zs, rows], sems[0].at[3], sems[1].at[3], to).start()
-                else:
-                    rcopy(zb.at[zs], zb.at[zs], sems[0].at[s], sems[1].at[s], to).start()
-
-    def y_copy(zs):
-        j = zs % 2
-        return rcopy(zb.at[zs], wt.at[y, x, j, core], sy.at[zs], ry.at[y, j], dev(z, x, zs // 2))
-
-    def y_send(zs):
-        j = zs % 2
-
+    def half(n):
+        return pl.ds(48 * n, 48)
+
+    def z_copy(way, zs, n, s):
+        p = zb.at[zs, half(n)]
+        to = dev((z + 1) % 8 if way == 0 else (z + 7) % 8, x, y)
+        return rcopy(p, p, sz.at[way, s, n], rz.at[way, s, n], to)
+
+    def z_start():
+        for n in range(2):
+            for way in range(2):
+                z_copy(way, z, n, 0).start()
+            y_send(z, n)
+
+    def y_copy(zs, n):
+        return rcopy(
+            zb.at[zs, half(n)], wt.at[y, x, zs % 2, core, half(n)],
+            sy.at[zs, n], ry.at[y, zs % 2, n], dev(z, x, zs // 2),
+        )
+
+    def y_send(zs, n):
         @pl.when(zs // 2 == y)
         def _():
-            pltpu.make_async_copy(zb.at[zs], wt.at[y, x, j, core], ry.at[y, j]).start()
+            pltpu.make_async_copy(
+                zb.at[zs, half(n)], wt.at[y, x, zs % 2, core, half(n)], ry.at[y, zs % 2, n]
+            ).start()
 
         @pl.when(zs // 2 != y)
         def _():
-            y_copy(zs).start()
-
-    def z_event(s):
-        z_send(s)
-        y_send((z + 8 - s) % 8)
-        if s in (1, 2, 3):
-            y_send((z + s) % 8)
+            y_copy(zs, n).start()
+
+    def z_event(s, n):
+        for way in range(2):
+            if s == 4 and way != n:
+                continue
+            zs = (z + 8 - s) % 8 if way == 0 else (z + s) % 8
+            z_copy(way, zs, n, s - 1).wait_recv()
+            if s < 3 or (s == 3 and way == n):
+                z_copy(way, zs, n, s).start()
+            y_send(zs, n)
 
     def dist(j):
         d = (2 * y + j + 8 - z) % 8
         return jnp.minimum(d, 8 - d)
 
     first = jnp.where(dist(0) < dist(1), 0, 1)
-
-    def piece(i, quarter, j):
-        return wt.at[(y + ORD[i]) % 4, quarter, j, core]
-
-    def up_copy(i, j):
-        p = piece(i, x, j)
-        return rcopy(p, p, sxu.at[j, i], rxu.at[j, i], dev(z, xup, y))
-
-    def dn_copy(i, j):
-        p = piece(i, x, j)
-        return rcopy(p, p, sxd.at[j, i], rxd.at[j, i], dev(z, xdn, y))
-
-    def pair_copy(which, i, j):
-        quarter = (x, xdn, xup, xop)[which]
-        p = wt.at[(y + order_at(i)) % 4, quarter, j, core]
-        return rcopy(p, p, s2d.at[which, j, i], r2d.at[which, j, i], dev(z, x, y, 1 - core))
+    second = 1 - first
 
     def order_at(i):
         if isinstance(i, int):
             return ORD[i]
         return jnp.where(i == 3, 2, jnp.where(i == 2, 3, i))
 
+    def piece(i, quarter, j):
+        return wt.at[(y + order_at(i)) % 4, quarter, j, core]
+
+    urgent = (2 * par, 2 * par + 1)
+    common = ((1, 3), (0, 2))
+    toward, source = (xup, xdn), (xdn, xup)
+
+    def x_copy(way, i, j):
+        p = piece(i, x, j)
+        return rcopy(p, p, sx.at[way, j, i], rx.at[way, j, i], dev(z, toward[way], y))
+
+    def pair_copy(which, i, j):
+        p = piece(i, (x, xdn, xup, xop)[which], j)
+        return rcopy(p, p, s2d.at[which, j, i], r2d.at[which, j, i], dev(z, x, y, 1 - core))
+
+    def pair_wait(which):
+        for j in range(2):
+            for i in range(4):
+                pair_copy(which, i, j).wait_recv()
+
+    def relay_copy(way, j):
+        p = piece(urgent[way], source[way], j)
+        return rcopy(p, p, srl.at[j, way], rrl.at[j, way], dev(z, toward[way], y))
+
+    def zpair_copy(w, j, mine=True):
+        i = (2 * par if mine else 2 * (1 - par)) + w % 2
+        p = piece(i, (xdn, xup, xop, xop)[w], j)
+        return rcopy(p, p, szp.at[j, w], rzp.at[j, w], dev(z + 1 - 2 * par, x, y))
+
     def x_send(j):
         for i in range(4):
-            yy = (y + ORD[i]) % 4
-            rcopy(
-                zb.at[0], wt.at[yy, x, j, core], sy.at[0], ry.at[yy, j], dev(z, x, (y + 1) % 4)
-            ).wait_recv()
-            up_copy(i, j).start()
-            dn_copy(i, j).start()
+            for n in range(2):
+                yy = (y + ORD[i]) % 4
+                rcopy(
+                    zb.at[0, half(n)], wt.at[yy, x, j, core, half(n)], sy.at[0, n],
+                    ry.at[yy, j, n], dev(z, x, (y + 1) % 4),
+                ).wait_recv()
+        for way in range(2):
+            x_copy(way, urgent[way], j).start()
+        for way in range(2):
+            x_copy(way, common[way][0], j).start()
+        for i in range(4):
             pair_copy(0, i, j).start()
 
     def x_stage(s):
@@ -151,56 +169,31 @@
             def _():
                 x_send(j)
 
-    def relay_copy(m, j):
-        i = 2 * par + m
-        quarter, to = (xdn, xup) if m == 0 else (xup, xdn)
-        p = wt.at[(y + order_at(i)) % 4, quarter, j, core]
-        return rcopy(p, p, srl.at[j, m], rrl.at[j, m], dev(z, to, y))
-
-    def x_event(n):
-        j = first if n < 4 else 1 - first
-        i = n % 4
-        up_copy(i, j).wait_recv()
-        pair_copy(1, i, j).start()
-        if i % 2 == 0:
-            @pl.when(par == i // 2)
-            def _():
-                relay_copy(0, j).start()
-        dn_copy(i, j).wait_recv()
-        pair_copy(2, i, j).start()
-        if i % 2 == 1:
-            @pl.when(par == i // 2)
-            def _():
-                relay_copy(1, j).start()
-
-    def zpair_copy(m, j, mine):
-        i = 2 * par + m if mine else 2 * (1 - par) + m
-        p = wt.at[(y + order_at(i)) % 4, xop, j, core]
-        return rcopy(p, p, szp.at[j, m], rzp.at[j, m], dev(z + 1 - 2 * par, x, y))
-
-    def opposite_event(n):
-        j = first if n < 2 else 1 - first
-        m = n % 2
-        p = wt.at[(y + order_at(2 * par + m)) % 4, xop, j, core]
-        rcopy(p, p, srl.at[j, m], rrl.at[j, m], dev(z, xup, y)).wait_recv()
-        zpair_copy(m, j, True).start()
-        pair_copy(3, 2 * par + m, j).start()
-
-    def zpair_event(n):
-        j = first if n < 2 else 1 - first
-        m = n % 2
-        zpair_copy(m, j, False).wait_recv()
-        pair_copy(3, 2 * (1 - par) + m, j).start()
-
-    def pair_wait(which):
-        for j in range(2):
-            for i in range(4):
-                pair_copy_in(which, i, j).wait_recv()
-
-    def pair_copy_in(which, i, j):
-        quarter = (x, xdn, xup, xop)[which]
-        p = wt.at[(y + ORD[i]) % 4, quarter, j, 1 - core]
-        return rcopy(p, p, s2d.at[which, j, i], r2d.at[which, j, i], dev(z, x, y, 1 - core))
+    def urgent_event(j):
+        for way in range(2):
+            x_copy(way, urgent[way], j).wait_recv()
+            relay_copy(way, j).start()
+            zpair_copy(way, j).start()
+            pair_copy(1 + way, urgent[way], j).start()
+
+    def common_start(j):
+        for way in range(2):
+            x_copy(way, common[way][1], j).start()
+
+    def common_event(n, j):
+        for way in range(2):
+            x_copy(way, common[way][n], j).wait_recv()
+            pair_copy(1 + way, common[way][n], j).start()
+
+    def opposite_event(j):
+        for way in range(2):
+            relay_copy(way, j).wait_recv()
+            zpair_copy(2 + way, j).start()
+            pair_copy(3, urgent[way], j).start()
+
+    def zpair_event(w, j):
+        zpair_copy(w, j, False).wait_recv()
+        pair_copy((1, 2, 3, 3)[w], 2 * (1 - par) + w % 2, j).start()
 
     yup, ydn, yop = (y + 1) % 4, (y + 3) % 4, (y + 2) % 4
 
@@ -216,6 +209,11 @@
     def h_relay(n):
         who, to = (ydn, yup) if n < 2 else (yup, ydn)
         return rcopy(chunk(who, n), chunk(who, n), shr.at[n], rhr.at[n], dev(z, x, to))
+
+    def h_relay_in(n):
+        return rcopy(
+            chunk(yop, n), chunk(yop, n), shr.at[n], rhr.at[n], dev(z, x, yup if n < 2 else ydn)
+        )
 
     def h_event(n):
         h_up(n).wait_recv()
@@ -232,7 +230,7 @@
     loads[0].wait()
     loads[1].wait()
     col = lax.broadcasted_iota(jnp.int32, (BLK, HD), 0).astype(F32)
-    for h in range(NH):
+    def contribs(h):
         r = rate[h]
         hs = slice(h * HD, (h + 1) * HD)
         kw = jnp.exp(-r * (BLK - 1.0 - col))
@@ -243,17 +241,20 @@
         c0[h] = a0.astype(BF16)
         loc[h] = (jnp.exp(jnp.full((1, HD), -r * BLK)) * a0 + a1).astype(BF16)
 
-    rx1[me] = loc[me]
+    for h in range(4):
+        contribs(h)
     loads[2].wait()
     pl.semaphore_wait(barrier, 17)
+    z_start()
+    for h in range(4, NH):
+        contribs(h)
+    rx1[me] = loc[me]
     sends = []
     for d in range(1, 8):
         to = (me + d) % 8
         cp = rcopy(loc.at[to], rx1.at[me], s1.at[d - 1], r1.at[me], (z * 8 + to, y))
         cp.start()
         sends.append(cp)
-    z_send(0)
-    y_send(z)
 
     loads[3].wait()
     loads[4].wait()
@@ -275,9 +276,9 @@
             u[rs, hs] = o
         gs[:, hs] = jax.nn.sigmoid(g[:, hs].astype(F32)) * gain[:, hs]
 
-    for h in range(3):
-        intra(h)
-
+    intra(0)
+    z_event(1, 0)
+    z_event(1, 1)
     for d in range(1, 8):
         p = (me + 8 - d) % 8
         rcopy(loc.at[0], rx1.at[p], s1.at[0], r1.at[p], (z * 8 + p, y)).wait_recv()
@@ -297,14 +298,19 @@
         def _():
             z_state(d).start()
 
-    z_event(1)
-    for h in range(3, 6):
-        intra(h)
-    z_event(2)
+    intra(1)
+    z_event(2, 0)
+    intra(2)
+    z_event(2, 1)
     x_stage(0)
+    intra(3)
+    intra(4)
+    z_event(3, 0)
+    intra(5)
+    z_event(3, 1)
     x_stage(1)
-    for h in range(6, NH):
-        intra(h)
+    intra(6)
+    intra(7)
 
     for i in range(7):
         @pl.when(i < z)
@@ -321,8 +327,10 @@
         cp.start()
         sends.append(cp)
 
-    z_event(3)
+    z_event(4, 0)
+    z_event(4, 1)
     x_stage(2)
+    x_stage(3)
 
     row = lax.broadcasted_iota(jnp.int32, (ROWS, HD), 0).astype(F32)
     for h in range(NH):
@@ -337,41 +345,43 @@
             h_up(h // 2).start()
             h_dn(h // 2).start()
 
-    z_event(4)
-    x_stage(3)
     x_stage(4)
 
-    x_event(0)
-    x_event(1)
+    urgent_event(first)
     pair_wait(0)
     unit(y, x, True)
-    x_event(2)
+    urgent_event(second)
+    common_start(first)
     h_event(0)
-    x_event(3)
+    common_event(0, first)
+    opposite_event(first)
+    common_start(second)
     h_event(1)
-    x_event(4)
+    common_event(0, second)
+    opposite_event(second)
     h_event(2)
-    x_event(5)
+    for j in (first, second):
+        for w in range(2):
+            zpair_event(w, j)
     h_event(3)
     unit(yup, x)
     unit(ydn, x)
-    x_event(6)
-    x_event(7)
+    common_event(1, first)
+    common_event(1, second)
     pair_wait(1)
     for who in (y, ydn, yup):
         unit(who, xdn, who is y)
     pair_wait(2)
     for who in (y, ydn, yup):
         unit(who, xup, who is y)
+    for w in range(2, 4):
+        zpair_event(w, first)
     for n in range(4):
-        opposite_event(n)
-    for n in range(4):
-        who, to = (yop, yup) if n < 2 else (yop, ydn)
-        rcopy(chunk(yop, n), chunk(yop, n), shr.at[n], rhr.at[n], dev(z, x, to)).wait_recv()
+        h_relay_in(n).wait_recv()
     for quarter in (x, xdn, xup):
         unit(yop, quarter)
-    for n in range(4):
-        zpair_event(n)
+    for w in range(2, 4):
+        zpair_event(w, second)
     pair_wait(3)
     for who in (y, ydn, yup, yop):
         unit(who, xop, who is y)
@@ -402,25 +412,25 @@
         @pl.when(z + d < 8)
         def _():
             z_state(d).wait_send()
-    for s in range(3):
-        rcopy(zb.at[0], zb.at[0], su.at[s], ru.at[s], dev((z + 1) % 8, x, y)).wait_send()
-        rcopy(zb.at[0], zb.at[0], sd.at[s], rd.at[s], dev((z + 7) % 8, x, y)).wait_send()
-    half = zb.at[0, pl.ds(0, 48)]
-    rcopy(half, half, su.at[3], ru.at[3], dev((z + 1) % 8, x, y)).wait_send()
-    rcopy(half, half, sd.at[3], rd.at[3], dev((z + 7) % 8, x, y)).wait_send()
+    for way in range(2):
+        for n in range(2):
+            for step in range(4 if way == n else 3):
+                z_copy(way, z, n, step).wait_send()
     for zs in range(8):
         @pl.when(zs // 2 != y)
         def _():
-            y_copy(zs).wait_send()
+            for n in range(2):
+                y_copy(zs, n).wait_send()
     for j in range(2):
+        for way in range(2):
+            x_copy(way, urgent[way], j).wait_send()
+            for n in range(2):
+                x_copy(way, common[way][n], j).wait_send()
+            relay_copy(way, j).wait_send()
         for i in range(4):
-            up_copy(i, j).wait_send()
-            dn_copy(i, j).wait_send()
             for which in range(4):
                 pair_copy(which, i, j).wait_send()
-        for m in range(2):
-            relay_copy(m, j).wait_send()
-            zpair_copy(m, j, True).wait_send()
+            zpair_copy(i, j).wait_send()
     for n in range(4):
         h_up(n).wait_send()
         h_dn(n).wait_send()
@@ -458,9 +468,8 @@
             pltpu.VMEM((4, ROWS, NH * HD), BF16),
             pltpu.VMEM((4, ROWS, 384), F32),
             dma((6,)), dma((7,)), dma((8,)), dma((7,)), dma((8,)), dma((7,)), dma((8,)),
-            dma((4,)), dma((4,)), dma((4,)), dma((4,)), dma((8,)), dma((4, 2)),
-            dma((2, 4)), dma((2, 4)), dma((2, 4)), dma((2, 4)),
-            dma((2, 2)), dma((2, 2)), dma((2, 2)), dma((2, 2)),
+            dma((2, 4, 2)), dma((2, 4, 2)), dma((8, 2)), dma((4, 2, 2)),
+            dma((2, 2, 4)), dma((2, 2, 4)), dma((2, 2)), dma((2, 2)), dma((2, 4)), dma((2, 4)),
             dma((4, 2, 4)), dma((4, 2, 4)),
             dma((4,)), dma((4,)), dma((4,)), dma((4,)), dma((4,)), dma((4,)),
         ],

time: 134 us -> 98 us (0.73)
  the two profiles are of different devices: /device:TPU:129 before, /device:TPU:1 now
where the time goes in v3:
time: 98 us; the launch traced here: 97.9 us
  Pallas kernels  95.2 us (97%)
  local copies, waits for them, and re-layouts  2.65 us (3%)
    pallas_call x1, Pallas kernels, body(): pl.pallas_call(kernel, out_shape=jax.ShapeDtypeStruct((ROWS, 1536), BF16)...  95.2 us
    unnamed x1, local copies, waits for them, and re-layouts  2.65 us

profile of v3, /device:TPU:1, one launch (start us, length us, event | category | flops | bytes accessed | tf_op | source)
XLA Modules:
  0.0 97.9 jit_solution(2879743920715610830)
XLA Ops:
  0.0 95.2 %shard_map.82 = bf16[512,1536]{1,0:T(8,128)(2,1)} custom-call(f32[8]{0:T(128)} %rate.1, f32[1,1024]{1,0:T(1,128)} %bitcast.3, f32[8,128,128]{2,1,0:T(8,128)} %init.1, bf16[512,1024]{1,0:T(8,128)(2,1)} %q_hbm.1, bf16[512,1024]{1,0:T(8,128)(2,1)} %k_hbm.1, bf16[512,1024]{1,0:T(8,128)(2,1)} %v_hbm.1, bf16[512,1024]{1,0:T(8,128)(2,1)} %g_hbm.1, ...), custom_call_target="tpu_custom_call" | custom-call | flops 8000000000 | bytes 6291456 | tf_op jit(solution)/shard_map/pallas_call | solution.py:446
  95.2 2.7 %copy.10 = bf16[512,1536]{1,0:T(8,128)(2,1)} copy(bf16[512,1536]{1,0:T(8,128)(2,1)} %shard_map.82) | data formatting | bytes 3145728

commit v4 on v3

--- a/solution.py
+++ b/solution.py
@@ -78,7 +78,7 @@
         for n in range(2):
             for way in range(2):
                 z_copy(way, z, n, 0).start()
-            y_send(z, n)
+            y_send(z, n, 0)
 
     def y_copy(zs, n):
         return rcopy(
@@ -86,14 +86,16 @@
             sy.at[zs, n], ry.at[y, zs % 2, n], dev(z, x, zs // 2),
         )
 
-    def y_send(zs, n):
-        @pl.when(zs // 2 == y)
-        def _():
-            pltpu.make_async_copy(
-                zb.at[zs, half(n)], wt.at[y, x, zs % 2, core, half(n)], ry.at[y, zs % 2, n]
-            ).start()
-
-        @pl.when(zs // 2 != y)
+    def y_send(zs, n, s):
+        rel = (y + 4 - zs // 2) % 4
+        if s % 2 == 1:
+            @pl.when(rel == 0)
+            def _():
+                pltpu.make_async_copy(
+                    zb.at[zs, half(n)], wt.at[y, x, zs % 2, core, half(n)], ry.at[y, zs % 2, n]
+                ).start()
+
+        @pl.when((rel == 1) if s % 2 == 1 else (rel >= 2))
         def _():
             y_copy(zs, n).start()
 
@@ -105,14 +107,13 @@
             z_copy(way, zs, n, s - 1).wait_recv()
             if s < 3 or (s == 3 and way == n):
                 z_copy(way, zs, n, s).start()
-            y_send(zs, n)
+            y_send(zs, n, s)
 
     def dist(j):
         d = (2 * y + j + 8 - z) % 8
         return jnp.minimum(d, 8 - d)
 
-    first = jnp.where(dist(0) < dist(1), 0, 1)
-    second = 1 - first
+    odd, even = 1 - par, par
 
     def order_at(i):
         if isinstance(i, int):
@@ -122,8 +123,13 @@
     def piece(i, quarter, j):
         return wt.at[(y + order_at(i)) % 4, quarter, j, core]
 
-    urgent = (2 * par, 2 * par + 1)
-    common = ((1, 3), (0, 2))
+    def mine(m, j):
+        return m + (0 if j is odd else 2 if j is even else 2 * ((par + j + 1) % 2))
+
+    def other(m, j):
+        return m + (2 if j is odd else 0 if j is even else 2 * ((par + j) % 2))
+
+    beside = (z + 1 - 2 * par, (z + 7 + 2 * par) % 8)
     toward, source = (xup, xdn), (xdn, xup)
 
     def x_copy(way, i, j):
@@ -134,66 +140,66 @@
         p = piece(i, (x, xdn, xup, xop)[which], j)
         return rcopy(p, p, s2d.at[which, j, i], r2d.at[which, j, i], dev(z, x, y, 1 - core))
 
-    def pair_wait(which):
-        for j in range(2):
-            for i in range(4):
+    def pair_wait(i):
+        for which in range(4):
+            for j in range(2):
                 pair_copy(which, i, j).wait_recv()
 
-    def relay_copy(way, j):
-        p = piece(urgent[way], source[way], j)
-        return rcopy(p, p, srl.at[j, way], rrl.at[j, way], dev(z, toward[way], y))
-
-    def zpair_copy(w, j, mine=True):
-        i = (2 * par if mine else 2 * (1 - par)) + w % 2
-        p = piece(i, (xdn, xup, xop, xop)[w], j)
-        return rcopy(p, p, szp.at[j, w], rzp.at[j, w], dev(z + 1 - 2 * par, x, y))
-
-    def x_send(j):
-        for i in range(4):
-            for n in range(2):
-                yy = (y + ORD[i]) % 4
-                rcopy(
-                    zb.at[0, half(n)], wt.at[yy, x, j, core, half(n)], sy.at[0, n],
-                    ry.at[yy, j, n], dev(z, x, (y + 1) % 4),
-                ).wait_recv()
-        for way in range(2):
-            x_copy(way, urgent[way], j).start()
-        for way in range(2):
-            x_copy(way, common[way][0], j).start()
-        for i in range(4):
-            pair_copy(0, i, j).start()
+    def relay_copy(way, j, own=True):
+        i = mine(way, j) if own else other(way, j)
+        p = piece(i, source[way], j)
+        return rcopy(p, p, srl.at[j, i], rrl.at[j, i], dev(z, toward[way], y))
+
+    def zn_copy(w, m, j):
+        p = piece(mine(m, j), (xdn, xup, x)[w], j)
+        return rcopy(p, p, szp.at[j, w, m], rzp.at[j, w, m], dev(beside[(w + m) % 2], x, y))
+
+    def ready(i, j):
+        yy = (y + order_at(i)) % 4
+        for n in range(2):
+            rcopy(
+                zb.at[0, half(n)], wt.at[yy, x, j, core, half(n)], sy.at[0, n],
+                ry.at[yy, j, n], dev(z, x, (y + 1) % 4),
+            ).wait_recv()
+
+    def x_early(s):
+        @pl.when(dist(odd) == s)
+        def _():
+            ready(0, odd)
+            for way in range(2):
+                x_copy(way, 0, odd).start()
+            zn_copy(2, 0, odd).start()
+            pair_copy(0, 0, odd).start()
 
     def x_stage(s):
-        for j in range(2):
-            @pl.when(dist(j) == s)
-            def _():
-                x_send(j)
-
-    def urgent_event(j):
-        for way in range(2):
-            x_copy(way, urgent[way], j).wait_recv()
-            relay_copy(way, j).start()
-            zpair_copy(way, j).start()
-            pair_copy(1 + way, urgent[way], j).start()
-
-    def common_start(j):
-        for way in range(2):
-            x_copy(way, common[way][1], j).start()
-
-    def common_event(n, j):
-        for way in range(2):
-            x_copy(way, common[way][n], j).wait_recv()
-            pair_copy(1 + way, common[way][n], j).start()
-
-    def opposite_event(j):
-        for way in range(2):
-            relay_copy(way, j).wait_recv()
-            zpair_copy(2 + way, j).start()
-            pair_copy(3, urgent[way], j).start()
-
-    def zpair_event(w, j):
-        zpair_copy(w, j, False).wait_recv()
-        pair_copy((1, 2, 3, 3)[w], 2 * (1 - par) + w % 2, j).start()
+        j = odd if s % 2 == 1 else even
+
+        @pl.when(dist(j) == s)
+        def _():
+            for m in range(s % 2, 2):
+                ready(mine(m, j), j)
+                for way in range(2):
+                    x_copy(way, mine(m, j), j).start()
+                zn_copy(2, m, j).start()
+                pair_copy(0, mine(m, j), j).start()
+
+    def x_event(j, m):
+        for way in (m, 1 - m):
+            x_copy(way, mine(m, j), j).wait_recv()
+            if way == m:
+                relay_copy(way, j).start()
+            zn_copy(way, m, j).start()
+            pair_copy(1 + way, mine(m, j), j).start()
+
+    def opposite_event(j, way, own=True):
+        relay_copy(way, j, own).wait_recv()
+        pair_copy(3, mine(way, j) if own else other(way, j), j).start()
+
+    def zn_event(w, m, j):
+        zn_copy(w, m, j).wait_recv()
+        if w == m:
+            relay_copy(w, j, False).start()
+        pair_copy((1, 2, 0)[w], other(m, j), j).start()
 
     yup, ydn, yop = (y + 1) % 4, (y + 3) % 4, (y + 2) % 4
 
@@ -277,8 +283,8 @@
         gs[:, hs] = jax.nn.sigmoid(g[:, hs].astype(F32)) * gain[:, hs]
 
     intra(0)
+    intra(1)
     z_event(1, 0)
-    z_event(1, 1)
     for d in range(1, 8):
         p = (me + 8 - d) % 8
         rcopy(loc.at[0], rx1.at[p], s1.at[0], r1.at[p], (z * 8 + p, y)).wait_recv()
@@ -298,17 +304,13 @@
         def _():
             z_state(d).start()
 
-    intra(1)
+    z_event(1, 1)
+    intra(2)
+    intra(3)
     z_event(2, 0)
-    intra(2)
+    intra(4)
+    intra(5)
     z_event(2, 1)
-    x_stage(0)
-    intra(3)
-    intra(4)
-    z_event(3, 0)
-    intra(5)
-    z_event(3, 1)
-    x_stage(1)
     intra(6)
     intra(7)
 
@@ -327,10 +329,12 @@
         cp.start()
         sends.append(cp)
 
+    x_early(1)
+    z_event(3, 0)
+    z_event(3, 1)
+    x_early(3)
     z_event(4, 0)
     z_event(4, 1)
-    x_stage(2)
-    x_stage(3)
 
     row = lax.broadcasted_iota(jnp.int32, (ROWS, HD), 0).astype(F32)
     for h in range(NH):
@@ -345,46 +349,53 @@
             h_up(h // 2).start()
             h_dn(h // 2).start()
 
+    x_stage(0)
+    x_stage(1)
+    x_event(odd, 0)
+    x_stage(2)
+    x_stage(3)
     x_stage(4)
-
-    urgent_event(first)
+    x_event(odd, 1)
+    zn_event(2, 0, even)
+    zn_event(0, 0, even)
+    zn_event(1, 0, even)
+    zn_event(2, 1, even)
+    x_event(even, 0)
+    zn_event(1, 1, even)
+    zn_event(0, 1, even)
+    x_event(even, 1)
+    opposite_event(odd, 0)
+    opposite_event(odd, 1)
+    h_event(0)
+    h_event(1)
+    opposite_event(even, 0, False)
+    zn_event(2, 0, odd)
+    zn_event(0, 0, odd)
+    zn_event(1, 0, odd)
+    h_event(2)
+    h_event(3)
+    zn_event(2, 1, odd)
+    zn_event(1, 1, odd)
+    zn_event(0, 1, odd)
+    opposite_event(even, 1, False)
     pair_wait(0)
-    unit(y, x, True)
-    urgent_event(second)
-    common_start(first)
-    h_event(0)
-    common_event(0, first)
-    opposite_event(first)
-    common_start(second)
-    h_event(1)
-    common_event(0, second)
-    opposite_event(second)
-    h_event(2)
-    for j in (first, second):
-        for w in range(2):
-            zpair_event(w, j)
-    h_event(3)
-    unit(yup, x)
-    unit(ydn, x)
-    common_event(1, first)
-    common_event(1, second)
+    for quarter in (x, xdn, xup, xop):
+        unit(y, quarter, True)
     pair_wait(1)
-    for who in (y, ydn, yup):
-        unit(who, xdn, who is y)
+    for quarter in (x, xdn, xup, xop):
+        unit(yup, quarter)
+    opposite_event(even, 0)
+    opposite_event(even, 1)
+    opposite_event(odd, 0, False)
+    opposite_event(odd, 1, False)
     pair_wait(2)
-    for who in (y, ydn, yup):
-        unit(who, xup, who is y)
-    for w in range(2, 4):
-        zpair_event(w, first)
+    for quarter in (x, xdn, xup, xop):
+        unit(ydn, quarter)
+    pair_wait(3)
     for n in range(4):
         h_relay_in(n).wait_recv()
-    for quarter in (x, xdn, xup):
+    for quarter in (x, xdn, xup, xop):
         unit(yop, quarter)
-    for w in range(2, 4):
-        zpair_event(w, second)
-    pair_wait(3)
-    for who in (y, ydn, yup, yop):
-        unit(who, xop, who is y)
 
     low = lax.broadcasted_iota(jnp.int32, (64, HD), 1) < 64
 
@@ -417,20 +428,24 @@
             for step in range(4 if way == n else 3):
                 z_copy(way, z, n, step).wait_send()
     for zs in range(8):
-        @pl.when(zs // 2 != y)
+        rel = (y + 4 - zs // 2) % 4
+        far = (z + zs) % 2
+
+        @pl.when(((far == 1) & (rel == 1)) | ((far == 0) & (rel >= 2)))
         def _():
             for n in range(2):
                 y_copy(zs, n).wait_send()
     for j in range(2):
         for way in range(2):
-            x_copy(way, urgent[way], j).wait_send()
-            for n in range(2):
-                x_copy(way, common[way][n], j).wait_send()
+            for m in range(2):
+                x_copy(way, mine(m, j), j).wait_send()
             relay_copy(way, j).wait_send()
+            relay_copy(way, j, False).wait_send()
+            for w in range(3):
+                zn_copy(w, way, j).wait_send()
         for i in range(4):
             for which in range(4):
                 pair_copy(which, i, j).wait_send()
-            zpair_copy(i, j).wait_send()
     for n in range(4):
         h_up(n).wait_send()
         h_dn(n).wait_send()
@@ -469,7 +484,7 @@
             pltpu.VMEM((4, ROWS, 384), F32),
             dma((6,)), dma((7,)), dma((8,)), dma((7,)), dma((8,)), dma((7,)), dma((8,)),
             dma((2, 4, 2)), dma((2, 4, 2)), dma((8, 2)), dma((4, 2, 2)),
-            dma((2, 2, 4)), dma((2, 2, 4)), dma((2, 2)), dma((2, 2)), dma((2, 4)), dma((2, 4)),
+            dma((2, 2, 4)), dma((2, 2, 4)), dma((2, 4)), dma((2, 4)), dma((2, 3, 2)), dma((2, 3, 2)),
             dma((4, 2, 4)), dma((4, 2, 4)),
             dma((4,)), dma((4,)), dma((4,)), dma((4,)), dma((4,)), dma((4,)),
         ],

time: 98 us -> 85 us (0.87)
  the two profiles are of different devices: /device:TPU:1 before, /device:TPU:19 now
where the time goes in v4:
time: 85 us; the launch traced here: 84.8 us
  Pallas kernels  82.2 us (97%)
  local copies, waits for them, and re-layouts  2.65 us (3%)
    pallas_call x1, Pallas kernels, body(): pl.pallas_call(kernel, out_shape=jax.ShapeDtypeStruct((ROWS, 1536), BF16)...  82.2 us
    unnamed x1, local copies, waits for them, and re-layouts  2.65 us

profile of v4, /device:TPU:19, one launch (start us, length us, event | category | flops | bytes accessed | tf_op | source)
XLA Modules:
  0.0 84.8 jit_solution(10988375348322181973)
XLA Ops:
  0.0 82.2 %shard_map.82 = bf16[512,1536]{1,0:T(8,128)(2,1)} custom-call(f32[8]{0:T(128)} %rate.1, f32[1,1024]{1,0:T(1,128)} %bitcast.3, f32[8,128,128]{2,1,0:T(8,128)} %init.1, bf16[512,1024]{1,0:T(8,128)(2,1)} %q_hbm.1, bf16[512,1024]{1,0:T(8,128)(2,1)} %k_hbm.1, bf16[512,1024]{1,0:T(8,128)(2,1)} %v_hbm.1, bf16[512,1024]{1,0:T(8,128)(2,1)} %g_hbm.1, ...), custom_call_target="tpu_custom_call" | custom-call | flops 8000000000 | bytes 6291456 | tf_op jit(solution)/shard_map/pallas_call | solution.py:461
  82.2 2.7 %copy.10 = bf16[512,1536]{1,0:T(8,128)(2,1)} copy(bf16[512,1536]{1,0:T(8,128)(2,1)} %shard_map.82) | data formatting | bytes 3145728

commit v5 on v4

--- a/solution.py
+++ b/solution.py
@@ -22,10 +22,10 @@
 
 def kernel(
     rate, gain, init, q_hbm, k_hbm, v_hbm, g_hbm, w_hbm, out,
-    q, k, v, g, u, gs, c0, loc, rx1, exc, tx2, rx2, tx3, rx3, zb, wt, hidg, acc,
+    q, k, v, g, u, gs, c0, loc, rx1, exc, tx2, rx2, tx3, rx3, zb, wt, hidg, acc, res,
     lsem, s1, r1, s2, r2, s3, r3,
     sz, rz, sy, ry, sx, rx, srl, rrl, szp, rzp, s2d, r2d,
-    shu, rhu, shd, rhd, shr, rhr,
+    shu, rhu, shd, rhd, shr, rhr, osem,
 ):
     c = lax.axis_index("ctx")
     y = lax.axis_index("head")
@@ -140,10 +140,9 @@
         p = piece(i, (x, xdn, xup, xop)[which], j)
         return rcopy(p, p, s2d.at[which, j, i], r2d.at[which, j, i], dev(z, x, y, 1 - core))
 
-    def pair_wait(i):
-        for which in range(4):
-            for j in range(2):
-                pair_copy(which, i, j).wait_recv()
+    def need(which, i):
+        for j in range(2):
+            pair_copy(which, i, j).wait_recv()
 
     def relay_copy(way, j, own=True):
         i = mine(way, j) if own else other(way, j)
@@ -333,8 +332,6 @@
     z_event(3, 0)
     z_event(3, 1)
     x_early(3)
-    z_event(4, 0)
-    z_event(4, 1)
 
     row = lax.broadcasted_iota(jnp.int32, (ROWS, HD), 0).astype(F32)
     for h in range(NH):
@@ -345,9 +342,12 @@
         at = u[:, hs] + jnp.exp(-rate[h] * (row + 1.0)) * dot(q[:, hs], rx3[h])
         scale = lax.rsqrt(jnp.mean(at * at, axis=-1, keepdims=True) + 1e-06)
         hidg[y, :, hs] = (at * scale * gs[:, hs]).astype(BF16)
-        if h % 2 == 1:
-            h_up(h // 2).start()
-            h_dn(h // 2).start()
+        if h == 7:
+            z_event(4, 0)
+            z_event(4, 1)
+            for n in range(4):
+                h_up(n).start()
+                h_dn(n).start()
 
     x_stage(0)
     x_stage(1)
@@ -355,6 +355,11 @@
     x_stage(2)
     x_stage(3)
     x_stage(4)
+    def units(i, which):
+        for n in which:
+            need(n, i)
+            unit((y, yup, ydn, yop)[i], (x, xdn, xup, xop)[n], i == 0)
+
     x_event(odd, 1)
     zn_event(2, 0, even)
     zn_event(0, 0, even)
@@ -364,59 +369,49 @@
     zn_event(1, 1, even)
     zn_event(0, 1, even)
     x_event(even, 1)
-    opposite_event(odd, 0)
-    opposite_event(odd, 1)
+    units(0, (0, 1, 2))
     h_event(0)
     h_event(1)
-    opposite_event(even, 0, False)
     zn_event(2, 0, odd)
     zn_event(0, 0, odd)
     zn_event(1, 0, odd)
     h_event(2)
-    h_event(3)
     zn_event(2, 1, odd)
     zn_event(1, 1, odd)
     zn_event(0, 1, odd)
+    h_event(3)
+    opposite_event(odd, 0)
+    opposite_event(odd, 1)
+    opposite_event(even, 0, False)
     opposite_event(even, 1, False)
-    pair_wait(0)
-    for quarter in (x, xdn, xup, xop):
-        unit(y, quarter, True)
-    pair_wait(1)
-    for quarter in (x, xdn, xup, xop):
-        unit(yup, quarter)
+    units(1, (0, 1, 2))
     opposite_event(even, 0)
     opposite_event(even, 1)
+    units(0, (3,))
+    units(1, (3,))
     opposite_event(odd, 0, False)
+    units(2, (0, 1, 2))
     opposite_event(odd, 1, False)
-    pair_wait(2)
-    for quarter in (x, xdn, xup, xop):
-        unit(ydn, quarter)
-    pair_wait(3)
-    for n in range(4):
-        h_relay_in(n).wait_recv()
-    for quarter in (x, xdn, xup, xop):
-        unit(yop, quarter)
-
-    low = lax.broadcasted_iota(jnp.int32, (64, HD), 1) < 64
-
-    def swap(t):
-        return pltpu.roll(t, 64, axis=1)
-
-    for pr in range(2):
-        for rb in range(8):
-            rs = slice(rb * 64, (rb + 1) * 64)
-            p0, p1, p2 = (acc[2 * pr, rs, n * HD : (n + 1) * HD] for n in range(3))
-            q0, q1, q2 = (acc[2 * pr + 1, rs, n * HD : (n + 1) * HD] for n in range(3))
-            sp1, sp2, sq0, sq1 = swap(p1), swap(p2), swap(q0), swap(q1)
-            tiles = (
-                (p0, jnp.where(low, p1, sq0), jnp.where(low, sq0, sq1)),
-                (jnp.where(low, sp1, sp2), jnp.where(low, sp2, q1), q2),
-            )
-            for j in range(2):
-                for n in range(3):
-                    at = j * 768 + pr * 384 + n * HD
-                    out[rs, at : at + HD] = tiles[j][n].astype(BF16)
-
+    units(2, (3,))
+    for n in range(3):
+        need(n, 3)
+    def part(quarter, n):
+        ks = slice(n * 256, (n + 1) * 256)
+        return dot(hidg[yop, :, ks], wt[yop, quarter, :, :, :, ks].reshape(384, 256), 1, 1)
+
+    h_relay_in(0).wait_recv()
+    h_relay_in(2).wait_recv()
+    for n, quarter in enumerate((x, xdn, xup, xop)):
+        if n == 3:
+            need(3, 3)
+        acc[quarter] += part(quarter, 0) + part(quarter, 2)
+    h_relay_in(1).wait_recv()
+    h_relay_in(3).wait_recv()
+    for n, quarter in enumerate((x, xdn, xup, xop)):
+        res[quarter] = (acc[quarter] + part(quarter, 1) + part(quarter, 3)).astype(BF16)
+        pltpu.make_async_copy(res.at[quarter], out.at[quarter], osem.at[n]).start()
+    for n, quarter in enumerate((x, xdn, xup, xop)):
+        pltpu.make_async_copy(res.at[quarter], out.at[quarter], osem.at[n]).wait()
     for cp in sends:
         cp.wait_send()
     for d in range(1, 8):
@@ -452,17 +447,43 @@
         h_relay(n).wait_send()
 
 
+def assemble(quarters, out):
+    low = lax.broadcasted_iota(jnp.int32, (64, HD), 1) < 64
+
+    def swap(t):
+        return pltpu.roll(t, 64, axis=1)
+
+    for pr in range(2):
+        for rb in range(8):
+            rs = slice(rb * 64, (rb + 1) * 64)
+            p0, p1, p2 = (
+                quarters[2 * pr, rs, n * HD : (n + 1) * HD].astype(F32) for n in range(3)
+            )
+            q0, q1, q2 = (
+                quarters[2 * pr + 1, rs, n * HD : (n + 1) * HD].astype(F32) for n in range(3)
+            )
+            sp1, sp2, sq0, sq1 = swap(p1), swap(p2), swap(q0), swap(q1)
+            tiles = (
+                (p0, jnp.where(low, p1, sq0), jnp.where(low, sq0, sq1)),
+                (jnp.where(low, sp1, sp2), jnp.where(low, sp2, q1), q2),
+            )
+            for j in range(2):
+                for n in range(3):
+                    at = j * 768 + pr * 384 + n * HD
+                    out[rs, at : at + HD] = tiles[j][n].astype(BF16)
+
+
 def body(
     query_rows, key_rows, value_rows, gate_rows, init_state, decay_rate, norm_gain, out_weight
 ):
     vm = pl.BlockSpec(memory_space=pltpu.VMEM)
     anyspace = pl.BlockSpec(memory_space=pl.ANY)
     dma = pltpu.SemaphoreType.DMA
-    return pl.pallas_call(
+    quarters = pl.pallas_call(
         kernel,
-        out_shape=jax.ShapeDtypeStruct((ROWS, 1536), BF16),
+        out_shape=jax.ShapeDtypeStruct((4, ROWS, 384), BF16),
         in_specs=[pl.BlockSpec(memory_space=pltpu.SMEM), vm] + [anyspace] * 6,
-        out_specs=vm,
+        out_specs=anyspace,
         scratch_shapes=[
             pltpu.VMEM((ROWS, NH * HD), BF16),
             pltpu.VMEM((ROWS, NH * HD), BF16),
@@ -482,11 +503,12 @@
             pltpu.VMEM((4, 4, 2, 2, 96, 1024), BF16),
             pltpu.VMEM((4, ROWS, NH * HD), BF16),
             pltpu.VMEM((4, ROWS, 384), F32),
+            pltpu.VMEM((4, ROWS, 384), BF16),
             dma((6,)), dma((7,)), dma((8,)), dma((7,)), dma((8,)), dma((7,)), dma((8,)),
             dma((2, 4, 2)), dma((2, 4, 2)), dma((8, 2)), dma((4, 2, 2)),
             dma((2, 2, 4)), dma((2, 2, 4)), dma((2, 4)), dma((2, 4)), dma((2, 3, 2)), dma((2, 3, 2)),
             dma((4, 2, 4)), dma((4, 2, 4)),
-            dma((4,)), dma((4,)), dma((4,)), dma((4,)), dma((4,)), dma((4,)),
+            dma((4,)), dma((4,)), dma((4,)), dma((4,)), dma((4,)), dma((4,)), dma((4,)),
         ],
         compiler_params=pltpu.CompilerParams(
             collective_id=0, has_side_effects=True, vmem_limit_bytes=60 * 2**20
@@ -498,6 +520,12 @@
         decay_rate, norm_gain[None, :], init_state, query_rows, key_rows, value_rows, gate_rows,
         out_weight.T,
     )
+    return pl.pallas_call(
+        assemble,
+        out_shape=jax.ShapeDtypeStruct((ROWS, 1536), BF16),
+        in_specs=[vm],
+        out_specs=vm,
+    )(quarters)
 
 
 def solution(mesh):

time: 85 us -> 83.6 us (0.984)
  the two profiles are of different devices: /device:TPU:19 before, /device:TPU:129 now
where the time goes in v5:
time: 83.6 us; the launch traced here: 83.5 us
  Pallas kernels  83.5 us (100%)
    pallas_call x1, Pallas kernels, body(): pl.pallas_call(kernel, out_shape=jax.ShapeDtypeStruct((4, ROWS, 384), BF1...  80.5 us
    pallas_call x1, Pallas kernels, body(): pl.pallas_call(assemble, out_shape=jax.ShapeDtypeStruct((ROWS, 1536), BF1...  2.99 us

profile of v5, /device:TPU:129, one launch (start us, length us, event | category | flops | bytes accessed | tf_op | source)
XLA Modules:
  0.0 83.5 jit_solution(9691782389218742777)
XLA Ops:
  0.0 80.5 %shard_map.82.quarters = bf16[4,512,384]{2,1,0:T(8,128)(2,1)} custom-call(f32[8]{0:T(128)} %rate.1, f32[1,1024]{1,0:T(1,128)} %bitcast.3, f32[8,128,128]{2,1,0:T(8,128)} %init.1, bf16[512,1024]{1,0:T(8,128)(2,1)} %q_hbm.1, bf16[512,1024]{1,0:T(8,128)(2,1)} %k_hbm.1, bf16[512,1024]{1,0:T(8,128)(2,1)} %v_hbm.1, bf16[512,1024]{1,0:T(8,128)(2,1)} %g_hbm.1, ...), custom_call_target="tpu_custom_call" | custom-call | flops 8000000000 | bytes 6291456 | tf_op jit(solution)/shard_map/pallas_call | solution.py:482
  80.5 3.0 %shard_map.83 = bf16[512,1536]{1,0:T(8,128)(2,1)} custom-call(bf16[4,512,384]{2,1,0:T(8,128)(2,1)} %shard_map.82.quarters), custom_call_target="tpu_custom_call" | custom-call | tf_op jit(solution)/shard_map/pallas_call | solution.py:523

commit v6 on v5

--- a/solution.py
+++ b/solution.py
@@ -284,6 +284,7 @@
     intra(0)
     intra(1)
     z_event(1, 0)
+    z_event(1, 1)
     for d in range(1, 8):
         p = (me + 8 - d) % 8
         rcopy(loc.at[0], rx1.at[p], s1.at[0], r1.at[p], (z * 8 + p, y)).wait_recv()
@@ -303,7 +304,6 @@
         def _():
             z_state(d).start()
 
-    z_event(1, 1)
     intra(2)
     intra(3)
     z_event(2, 0)

time: 83.6 us -> 82.8 us (level)
  Pallas kernels: 83.5 us -> 82.3 us
    pallas_call x1, Pallas kernels: 80.5 us -> 79.3 us  [body(): pl.pallas_call(kernel, out_shape=jax.ShapeDtypeStruct((4, ROWS, 384), BF1...]
where the time goes in v6:
time: 82.8 us; the launch traced here: 82.3 us
  Pallas kernels  82.3 us (99%)
    pallas_call x1, Pallas kernels, body(): pl.pallas_call(kernel, out_shape=jax.ShapeDtypeStruct((4, ROWS, 384), BF1...  79.3 us
    pallas_call x1, Pallas kernels, body(): pl.pallas_call(assemble, out_shape=jax.ShapeDtypeStruct((ROWS, 1536), BF1...  2.99 us

profile of v6, /device:TPU:129, one launch (start us, length us, event | category | flops | bytes accessed | tf_op | source)
XLA Modules:
  0.0 82.3 jit_solution(13262357604810216212)
XLA Ops:
  0.0 79.3 %shard_map.82.quarters = bf16[4,512,384]{2,1,0:T(8,128)(2,1)} custom-call(f32[8]{0:T(128)} %rate.1, f32[1,1024]{1,0:T(1,128)} %bitcast.3, f32[8,128,128]{2,1,0:T(8,128)} %init.1, bf16[512,1024]{1,0:T(8,128)(2,1)} %q_hbm.1, bf16[512,1024]{1,0:T(8,128)(2,1)} %k_hbm.1, bf16[512,1024]{1,0:T(8,128)(2,1)} %v_hbm.1, bf16[512,1024]{1,0:T(8,128)(2,1)} %g_hbm.1, ...), custom_call_target="tpu_custom_call" | custom-call | flops 8000000000 | bytes 6291456 | tf_op jit(solution)/shard_map/pallas_call | solution.py:482
  79.4 3.0 %shard_map.83 = bf16[512,1536]{1,0:T(8,128)(2,1)} custom-call(bf16[4,512,384]{2,1,0:T(8,128)(2,1)} %shard_map.82.quarters), custom_call_target="tpu_custom_call" | custom-call | tf_op jit(solution)/shard_map/pallas_call | solution.py:523
